TPU v7x, 32 devices: a whole 2x2x4 slice. The times are simulated.
32 devices in a mesh: band: 4 (over y, x), dom: 8 (over z, core).
Axes of the slice: x: 2, y: 2, z: 4, core: 2. Of those that a mesh axis runs over, the one named last changes fastest.
Arguments:
- partial_density: float32 [4, 48, 96, 128], P('band', 'dom'), may hold values from 0.002 to 0.1
- moments: bfloat16 [9, 64], P(None, 'dom'), may hold values from 0.0099487305 to 0.099609375
- shape_functions: bfloat16 [64, 9, 6912], P('dom'), may hold values from 0.099609375 to 1
- sphere_offsets: int32 [3, 64], P(None, 'dom'), may hold values from 0 to 232, as said below
- owned_count: int32 [8], P('dom'), may hold values from 1 to 8, as said below
Outputs:
- potential: float32 [48, 96, 128], P('dom')
Inputs may be any that keep to these rules, and one draw needn't show every extreme that they name: `sphere_offsets`: row 0 lies in 0 to 11, and in 0 to 0 for the last slab; row 1 in 0 to 168; row 2 in 0 to 232; each upper end is reached. `owned_count`: some slab owns exactly 8 atoms.
All inputs are finite; a program needn't handle non-finite values.
Results may differ from a plain program's by a relative error of at most 0.0003.
Values sent between devices are 32-bit elements; how exact they have to be, the bound alone decides.
A program may use at most 64 MiB of HBM per device.

v0:
```python
import jax
import jax.numpy as jnp
from jax import lax
from jax.sharding import PartitionSpec as P

SBX = 12
SBY = 24
SBZ = 24


kappa_pbe = 0.804
mu_pbe = 0.2195
exchange_prefactor = -0.75 * (3.0 / 3.141592653589793) ** (1.0 / 3.0)
gradient_scale = 4.0 * (3.0 * 3.141592653589793**2) ** (2.0 / 3.0)
half_inverse = 0.5 / 0.2


def from_behind(block, axis, distance):
    devices = range(lax.axis_size(axis))
    route = [(i - distance, i) for i in devices if i - distance in devices]
    return lax.ppermute(block, axis, route)


def extended_2(cells, sides, width):
    for axis, dim in sides:
        count = lax.axis_size(axis)
        ends = count - 1
        head = lax.slice_in_dim(cells, 0, width, axis=dim)
        tail = lax.slice_in_dim(cells, cells.shape[dim] - width, cells.shape[dim], axis=dim)
        cells = jnp.concatenate(
            [
                lax.ppermute(tail, axis, [(i, (i + 1) % count) for i in range(ends)]),
                cells,
                lax.ppermute(head, axis, [((i + 1) % count, i) for i in range(ends)]),
            ],
            axis=dim,
        )
    return cells


def refine(extended, direction):
    length = extended.shape[direction] - 2
    lower_cells = lax.slice_in_dim(extended, 0, length, axis=direction)
    middle_cells = lax.slice_in_dim(extended, 1, length + 1, axis=direction)
    upper_cells = lax.slice_in_dim(extended, 2, length + 2, axis=direction)
    even_cells = 0.75 * middle_cells + 0.25 * lower_cells
    odd_cells = 0.75 * middle_cells + 0.25 * upper_cells
    joined = jnp.stack([even_cells, odd_cells], axis=direction + 1)
    target = list(middle_cells.shape)
    target[direction] = 2 * length
    return joined.reshape(target)


def restrict(extended, direction):
    doubled = extended.shape[direction] - 2
    halved = doubled // 2

    def paired(start):
        piece = lax.slice_in_dim(extended, start, start + doubled, axis=direction)
        target = list(piece.shape)
        target[direction : direction + 1] = [halved, 2]
        return piece.reshape(target)

    centre = paired(1)
    outer_low = lax.index_in_dim(paired(0), 0, direction + 1, keepdims=False)
    outer_high = lax.index_in_dim(paired(2), 1, direction + 1, keepdims=False)
    first_half = lax.index_in_dim(centre, 0, direction + 1, keepdims=False)
    second_half = lax.index_in_dim(centre, 1, direction + 1, keepdims=False)
    return 0.125 * outer_low + 0.375 * (first_half + second_half) + 0.125 * outer_high


def exchange_parts(density, sigma):
    cube_root = jnp.cbrt(density)
    four_thirds = density * cube_root
    reduced = sigma / (gradient_scale * four_thirds * four_thirds)
    damped = 1.0 + mu_pbe * reduced / kappa_pbe
    enhance = 1.0 + kappa_pbe - kappa_pbe / damped
    slope = mu_pbe / (damped * damped)
    by_density = (
        exchange_prefactor * cube_root * (4.0 / 3.0 * enhance - 8.0 / 3.0 * reduced * slope)
    )
    by_sigma = exchange_prefactor * slope / (gradient_scale * four_thirds)
    return (by_density, by_sigma)


def selector(offset, extent, length):
    inside = jnp.arange(extent)
    target = jnp.arange(length)
    return (offset[:, None, None] + inside[None, :, None] == target[None, None, :]).astype(
        jnp.float32
    )


def place(blocks, row_offset, col_offset, depth_offset, rows_out, cols_out, depth_out):
    slot_count = blocks.shape[0]
    cube = blocks.reshape(slot_count, SBX, SBY, SBZ)
    pick_rows = selector(row_offset, SBX, rows_out)
    pick_cols = selector(col_offset, SBY, cols_out)
    pick_depth = selector(depth_offset, SBZ, depth_out)
    highest = lax.Precision.HIGHEST
    section_rows = jnp.einsum("sabc,sax->sxbc", cube, pick_rows, precision=highest)
    section_cols = jnp.einsum("sxbc,sby->sxcy", section_rows, pick_cols, precision=highest)
    return jnp.einsum("sxcy,scz->xyz", section_cols, pick_depth, precision=highest)


def transform(coarse, spheres, coarse_rim, face_rim, fine_rim):
    fine = coarse_rim(coarse)
    for direction in range(3):
        fine = refine(fine, direction)
    density = fine + spheres
    extended = face_rim(density[None])[0]
    grad_x = (extended[2:, 1:-1, 1:-1] - extended[:-2, 1:-1, 1:-1]) * half_inverse
    grad_y = (extended[1:-1, 2:, 1:-1] - extended[1:-1, :-2, 1:-1]) * half_inverse
    grad_z = (extended[1:-1, 1:-1, 2:] - extended[1:-1, 1:-1, :-2]) * half_inverse
    sigma = grad_x * grad_x + grad_y * grad_y + grad_z * grad_z
    by_density, by_sigma = exchange_parts(density, sigma)
    flux = jnp.stack([2.0 * by_sigma * grad_x, 2.0 * by_sigma * grad_y, 2.0 * by_sigma * grad_z])
    flux_ext = face_rim(flux)
    spread = flux_ext[0, 2:, 1:-1, 1:-1] - flux_ext[0, :-2, 1:-1, 1:-1]
    spread = spread + flux_ext[1, 1:-1, 2:, 1:-1] - flux_ext[1, 1:-1, :-2, 1:-1]
    spread = spread + flux_ext[2, 1:-1, 1:-1, 2:] - flux_ext[2, 1:-1, 1:-1, :-2]
    fine_potential = by_density - spread * half_inverse
    result = fine_rim(fine_potential)
    for direction in range(3):
        result = restrict(result, direction)
    return result


def body(partial_density, moments, shape_functions, sphere_offsets, owned_count):
    coarse_x = partial_density.shape[1]
    coarse_y = partial_density.shape[2]
    fine_x = 2 * coarse_x
    fine_y = 2 * coarse_y
    fine_z = 2 * partial_density.shape[3]
    slot_total = moments.shape[1]
    live = (jnp.arange(slot_total) < owned_count[0]).astype(jnp.bfloat16)
    blocks = jnp.einsum(
        "ls,slk->sk", moments * live[None, :], shape_functions, preferred_element_type=jnp.float32
    )
    buffer = place(
        blocks,
        sphere_offsets[0],
        sphere_offsets[1],
        sphere_offsets[2],
        fine_x + SBX,
        fine_y,
        fine_z,
    )
    own_spheres = buffer[:fine_x]
    arrived = from_behind(buffer[fine_x:], "dom", 1)
    own_spheres = own_spheres.at[:SBX].add(arrived)
    coarse = lax.psum(partial_density, "band")[0]

    def coarse_rim(field):
        padded = extended_2(field, (("dom", 0),), 1)
        return jnp.pad(padded, ((0, 0), (1, 1), (1, 1)))

    def face_rim(field):
        padded = extended_2(field, (("dom", 1),), 1)
        return jnp.pad(padded, ((0, 0), (0, 0), (1, 1), (1, 1)))

    def fine_rim(field):
        padded = extended_2(field, (("dom", 0),), 1)
        return jnp.pad(padded, ((0, 0), (1, 1), (1, 1)))

    return transform(coarse, own_spheres, coarse_rim, face_rim, fine_rim)


def solution(mesh):
    return jax.shard_map(
        body,
        mesh=mesh,
        in_specs=(
            P("band", "dom", None, None),
            P(None, "dom"),
            P("dom", None, None),
            P(None, "dom"),
            P("dom"),
        ),
        out_specs=P("dom", None, None),
        check_vma=False,
    )
```

profile of v0, /device:TPU:0, one launch (start us, length us, event | category | flops | bytes accessed | tf_op | source)
XLA Modules:
  0.0 193.4 jit_solution(16997898254485083587)
XLA Ops:
  7.3 0.8 slice_bitcast_fusion.6
  9.4 0.8 reshape.196
  10.4 1.3 fusion.32
  11.7 2.2 %fusion.21 = f32[8,24,24,192]{3,2,0,1:T(8,128)S(1)} fusion(f32[8,24,24,24]{3,1,2,0:T(8,128)S(1)} %fusion.32, s32[8,24]{1,0:T(8,128)S(1)} %get-tuple-element.56), kind=kOutput, calls=%fused_computation.60 | convolution fusion | flops 254840832 | bytes 3982080 | tf_op jit(solution)/shard_map/sxbc,sby->sxcy/dot_general | solution.py:102
  13.9 4.7 %convolution_bitcast_fusion = f32[24,192,256]{2,1,0:T(8,128)S(1)} fusion(f32[8,24,24,192]{3,2,0,1:T(8,128)S(1)} %fusion.21, s32[8,24]{1,0:T(8,128)S(1)} %get-tuple-element.55), kind=kOutput, calls=%fused_computation.67 | convolution fusion | flops 2717958144 | bytes 8258304 | tf_op jit(solution)/shard_map/sxcy,scz->xyz/dot_general | solution.py:103
  18.6 1.6 slice.263
  20.2 1.3 copy-done.3
  21.5 3.8 %collective-permute-start.2 = (f32[12,192,256]{2,1,0:T(8,128)}, f32[12,192,256]{2,1,0:T(8,128)}, u32[]{:S(2)}, u32[]{:S(2)}) collective-permute-start(f32[12,192,256]{2,1,0:T(8,128)} %slice.263), channel_id=1, source_target_pairs={{0,1},{1,2},{2,3},{3,4},{4,5},{5,6},{6,7},{8,9},{9,10},{10,11},{11... | collective-permute-start | bytes 7077896 | tf_op jit(solution)/shard_map/ppermute | solution.py:21
  25.3 0.9 copy.8
  26.3 45.3 %all-reduce.6.cloned.1.call-done = f32[1,6,96,128]{2,3,1,0:T(8,128)} async-done(((f32[1,6,96,128]{2,3,1,0:T(8,128)}), f32[1,6,96,128]{2,3,1,0:T(8,128)}) %all-reduce.6.cloned.1.call-update) | async-done | bytes 294928 | tf_op jit(solution)/shard_map/psum | solution.py:152
  71.6 0.9 slice_bitcast_fusion.5
  72.5 1.3 collective-permute-start
  73.8 1.5 collective-permute-start.1
  75.3 3.4 %collective-permute-done.1 = f32[1,96,128]{1,2,0:T(8,128)S(1)} collective-permute-done((f32[1,96,128]{1,2,0:T(8,128)S(1)}, f32[1,96,128]{1,2,0:T(8,128)S(1)}, u32[]{:S(2)}, u32[]{:S(2)}) %collective-permute-start.1) | collective-permute-done | bytes 49184 | tf_op jit(solution)/shard_map/ppermute | solution.py:34
  78.7 1.2 select_maximum_fusion.8
  80.6 2.6 %copy.11 = f32[12,96,2,130]{3,2,1,0:T(2,128)} copy(f32[12,96,2,130]{1,3,0,2:T(8,128)S(1)} %pad_maximum_fusion.7) | data formatting | bytes 2396160 | tf_op jit(solution)/shard_map/stack | solution.py:48
  83.2 3.1 %reshape.194 = f32[12,192,130]{2,1,0:T(8,128)S(1)} reshape(f32[12,96,2,130]{3,2,1,0:T(2,128)} %copy.11) | data formatting | bytes 2396160 | tf_op jit(solution)/shard_map/reshape | solution.py:51
  87.0 1.6 pad_maximum_fusion.6
  88.6 4.0 %copy.12 = f32[12,192,128,2]{1,3,2,0:T(2,128)S(1)} copy(f32[12,192,128,2]{2,1,0,3:T(8,128)} %pad_maximum_fusion.6) | data formatting | bytes 4718592 | tf_op jit(solution)/shard_map/stack | solution.py:48
  92.6 3.4 %reshape.195 = f32[12,192,256]{1,2,0:T(8,128)} reshape(f32[12,192,128,2]{1,3,2,0:T(2,128)S(1)} %copy.12) | data formatting | bytes 4718592 | tf_op jit(solution)/shard_map/reshape | solution.py:51
  96.1 2.3 %copy.13 = f32[12,192,256]{2,1,0:T(8,128)S(1)} copy(f32[12,192,256]{1,2,0:T(8,128)} %reshape.195) | data formatting | bytes 4718592 | tf_op jit(solution)/shard_map/reshape | solution.py:51
  98.4 2.8 %fusion.20 = f32[12,192,256]{2,1,0:T(8,128)S(1)} fusion(f32[12,192,256]{2,1,0:T(8,128)S(1)} %copy.13, f32[12,192,256]{2,1,0:T(8,128)} %collective-permute-done.2, f32[24,192,256]{2,1,0:T(8,128)} %copy-done.3), kind=kLoop, calls=%fused_computation.58 | loop fusion | flops 1179648 | bytes 9437184 | tf_op jit(solution)/shard_map/add | solution.py:110
  101.3 4.8 %collective-permute-start.3 = (f32[1,1,192,256]{3,2,1,0:T(8,128)S(1)}, f32[1,1,192,256]{3,2,1,0:T(8,128)S(1)}, u32[]{:S(2)}, u32[]{:S(2)}) collective-permute-start(f32[1,1,192,256]{3,2,1,0:T(8,128)S(1)} %get-tuple-element.36), channel_id=1, source_target_pairs={{0,1},{1,2},{2,3},{3,4},{4,5},{5,6},{6,7},{8,9},{9,10},{10,11},{11... | collective-permute-start | bytes 589832 | tf_op jit(solution)/shard_map/ppermute | solution.py:32
  106.2 1.3 collective-permute-start.4
  107.5 2.0 %collective-permute-done.4 = f32[1,1,192,256]{3,2,1,0:T(8,128)S(1)} collective-permute-done((f32[1,1,192,256]{3,2,1,0:T(8,128)S(1)}, f32[1,1,192,256]{3,2,1,0:T(8,128)S(1)}, u32[]{:S(2)}, u32[]{:S(2)}) %collective-permute-start.4) | collective-permute-done | bytes 196640 | tf_op jit(solution)/shard_map/ppermute | solution.py:34
  109.5 2.6 %fusion.3 = f32[14,194,258]{2,1,0:T(8,128)S(1)} fusion(f32[1,1,192,256]{3,2,1,0:T(8,128)S(1)} %collective-permute-done.4, f32[1,12,192,256]{3,2,1,0:T(8,128)S(1)} %bitcast.104, f32[1,1,192,256]{3,2,1,0:T(8,128)S(1)} %collective-permute-done.3), kind=kLoop, calls=%fused_computation.22 | loop fusion | flops 10510920 | bytes 5555424 | tf_op jit(solution)/shard_map/squeeze | solution.py:111
  112.1 6.0 %multiply_bitcast_fusion.2 = (f32[1,12,192,256]{3,2,1,0:T(8,128)S(1)}, f32[12,192,256]{2,1,0:T(8,128)S(1)}) fusion(f32[14,194,258]{2,1,0:T(8,128)S(1)} %fusion.3, f32[12,192,256]{2,1,0:T(8,128)S(1)} %fusion.20), kind=kLoop, calls=%fused_computation.64 | loop fusion | flops 13565952 | bytes 21233664 | tf_op jit(solution)/shard_map/stack | solution.py:117
  118.1 4.4 %multiply_bitcast_fusion.1 = (f32[1,12,192,256]{3,2,1,0:T(8,128)S(1)}, f32[1,12,192,256]{3,2,1,0:T(8,128)S(1)}) fusion(f32[14,194,258]{2,1,0:T(8,128)S(1)} %fusion.3, f32[12,192,256]{2,1,0:T(8,128)S(1)} %fusion.20, f32[12,192,256]{2,1,0:T(8,128)S(1)} %get-tuple-element.26), kind=kLoop, calls=%fused_computation.63 | loop fusion | flops 8847360 | bytes 18874368 | tf_op jit(solution)/shard_map/stack | solution.py:117
  122.7 5.6 %collective-permute-start.6 = (f32[3,1,192,256]{3,2,1,0:T(8,128)S(1)}, f32[3,1,192,256]{3,2,1,0:T(8,128)S(1)}, u32[]{:S(2)}, u32[]{:S(2)}) collective-permute-start(f32[3,1,192,256]{3,2,1,0:T(8,128)S(1)} %get-tuple-element.29), channel_id=1, source_target_pairs={{0,1},{1,2},{2,3},{3,4},{4,5},{5,6},{6,7},{8,9},{9,10},{10,11},{11... | collective-permute-start | bytes 1769480 | tf_op jit(solution)/shard_map/ppermute | solution.py:32
  128.3 1.5 collective-permute-start.5
  129.8 2.3 %collective-permute-done.5 = f32[3,1,192,256]{3,2,1,0:T(8,128)S(1)} collective-permute-done((f32[3,1,192,256]{3,2,1,0:T(8,128)S(1)}, f32[3,1,192,256]{3,2,1,0:T(8,128)S(1)}, u32[]{:S(2)}, u32[]{:S(2)}) %collective-permute-start.5) | collective-permute-done | bytes 589856 | tf_op jit(solution)/shard_map/ppermute | solution.py:34
  132.2 0.8 copy-done.5
  133.0 9.4 %select_maximum_fusion = f32[3,14,194,258]{3,2,1,0:T(8,128)S(1)} fusion(f32[3,1,192,256]{3,2,1,0:T(8,128)S(1)} %collective-permute-done.5, f32[3,1,192,256]{3,2,1,0:T(8,128)S(1)} %collective-permute-done.6, f32[1,12,192,256]{3,2,1,0:T(8,128)S(1)} %get-tuple-element.28, f32[1,12,192,256]{3,2,1,0:T(8,128)S(1)} %get-tuple-element.27, ...), kind=kLoop, calls=%fused_computation.4 | loop fusion | flops 44145864 | bytes 16666272 | tf_op jit(solution)/shard_map/concatenate | solution.py:30
  142.4 7.0 %fusion.11 = f32[12,192,256]{2,1,0:T(8,128)} fusion(f32[12,192,256]{2,1,0:T(8,128)S(1)} %fusion.20, f32[3,14,194,258]{3,2,1,0:T(8,128)S(1)} %select_maximum_fusion, f32[3,1,192,256]{3,2,1,0:T(8,128)} %copy-done.4, f32[1,12,192,256]{3,2,1,0:T(8,128)S(1)} %get-tuple-element.28, f32[1,12,192,256]{3,2,1,0:T(8,128)S(1)} %get-tuple-element.27, ...), kind=kLoop, calls=%fused_computation.35 | loop fusion | flops 14745600 | bytes 24772608 | tf_op jit(solution)/shard_map/sub | solution.py:122
  149.5 1.0 fusion.67
  150.5 9.2 %collective-permute-start.7 = (f32[1,192,256]{2,1,0:T(8,128)S(1)}, f32[1,192,256]{2,1,0:T(8,128)S(1)}, u32[]{:S(2)}, u32[]{:S(2)}) collective-permute-start(f32[1,192,256]{2,1,0:T(8,128)S(1)} %get-tuple-element.34), channel_id=1, source_target_pairs={{0,1},{1,2},{2,3},{3,4},{4,5},{5,6},{6,7},{8,9},{9,10},{10,11},{11... | collective-permute-start | bytes 589832 | tf_op jit(solution)/shard_map/ppermute | solution.py:32
  159.7 1.3 collective-permute-start.8
  161.0 2.0 %collective-permute-done.8 = f32[1,192,256]{2,1,0:T(8,128)S(1)} collective-permute-done((f32[1,192,256]{2,1,0:T(8,128)S(1)}, f32[1,192,256]{2,1,0:T(8,128)S(1)}, u32[]{:S(2)}, u32[]{:S(2)}) %collective-permute-start.8) | collective-permute-done | bytes 196640 | tf_op jit(solution)/shard_map/ppermute | solution.py:34
  163.1 4.1 %select_maximum_fusion.4 = f32[14,194,258]{2,1,0:T(8,128)S(1)} fusion(f32[1,192,256]{2,1,0:T(8,128)S(1)} %collective-permute-done.8, f32[12,192,256]{2,1,0:T(8,128)} %fusion.11, f32[1,192,256]{2,1,0:T(8,128)S(1)} %collective-permute-done.7), kind=kLoop, calls=%fused_computation.19 | loop fusion | flops 10510920 | bytes 5555424 | tf_op jit(solution)/shard_map/concatenate | solution.py:30
  167.2 2.5 %fusion.66 = (f32[12,194,258]{2,1,0:T(8,128)S(1)}, f32[12,194,258]{2,1,0:T(8,128)S(1)}, f32[12,194,258]{2,1,0:T(8,128)}) fusion(f32[14,194,258]{2,1,0:T(8,128)S(1)} %select_maximum_fusion.4), kind=kLoop, calls=%fused_computation.151 | loop fusion | bytes 14414976 | tf_op jit(solution)/shard_map/slice | solution.py:59
  169.7 1.9 %fusion.25 = f32[6,194,258]{2,1,0:T(8,128)S(1)} fusion(f32[6,2,194,258]{3,2,1,0:T(8,128)} %bitcast.109, f32[6,2,194,258]{3,2,1,0:T(8,128)S(1)} %bitcast.105, f32[6,2,194,258]{3,2,1,0:T(8,128)S(1)} %bitcast.108), kind=kLoop, calls=%fused_computation.71 | loop fusion | flops 1801872 | bytes 6006240 | tf_op jit(solution)/shard_map/add | solution.py:69
  171.6 1.6 fusion.69
  173.2 3.2 %reshape.200 = f32[6,96,2,258]{3,2,1,0:T(2,128)} reshape(f32[6,192,258]{2,1,0:T(8,128)} %get-tuple-element.40) | data formatting | bytes 2377728 | tf_op jit(solution)/shard_map/reshape | solution.py:62
  176.4 2.3 %reshape.202 = f32[6,96,2,258]{3,2,1,0:T(2,128)} reshape(f32[6,192,258]{2,1,0:T(8,128)S(1)} %get-tuple-element.41) | data formatting | bytes 2377728 | tf_op jit(solution)/shard_map/reshape | solution.py:62
  178.7 1.1 reshape.201
  179.7 3.9 %fusion.38 = f32[6,96,1,258]{3,2,1,0:T(1,128)S(1)} fusion(f32[6,96,2,258]{3,2,1,0:T(2,128)} %reshape.202, f32[6,96,2,258]{3,2,1,0:T(2,128)S(1)} %reshape.201, f32[6,96,2,258]{3,2,1,0:T(2,128)} %reshape.200), kind=kLoop, calls=%fused_computation.92 | loop fusion | flops 891648 | bytes 2972160 | tf_op jit(solution)/shard_map/add | solution.py:69
  184.6 1.1 fusion.52
  185.7 0.9 copy.19
  (34 shorter events, 4.0 us)
Async XLA Ops:
  6.5 2.4 %copy-start = (bf16[8,9,6912]{2,0,1:T(8,128)(2,1)S(1)}, bf16[8,9,6912]{2,0,1:T(8,128)(2,1)}, u32[]{:S(2)}) copy-start(bf16[8,9,6912]{2,0,1:T(8,128)(2,1)} %param.11) | copy-start | bytes 2985988
  6.5 65.1 %all-reduce.6.cloned.1.call-start = ((), (), s32[]{:S(2)}) async-start(), calls=%async_computation | async-start | bytes 786432 | tf_op jit(solution)/shard_map/psum | solution.py:152
  18.6 2.9 %copy-start.3 = (f32[24,192,256]{2,1,0:T(8,128)}, f32[24,192,256]{2,1,0:T(8,128)S(1)}, u32[]{:S(2)}) copy-start(f32[24,192,256]{2,1,0:T(8,128)S(1)} %convolution_bitcast_fusion) | copy-start | bytes 14155780
  18.6 6.7 %copy-start.6 = (f32[1,6,96,128]{3,2,1,0:T(8,128)S(1)}, f32[1,6,96,128]{3,2,1,0:T(8,128)}, u32[]{:S(2)}) copy-start(f32[1,6,96,128]{3,2,1,0:T(8,128)} %param.9) | copy-start | bytes 884740
  21.5 77.0 %collective-permute-start.2 = (f32[12,192,256]{2,1,0:T(8,128)}, f32[12,192,256]{2,1,0:T(8,128)}, u32[]{:S(2)}, u32[]{:S(2)}) collective-permute-start(f32[12,192,256]{2,1,0:T(8,128)} %slice.263), channel_id=1, source_target_pairs={{0,1},{1,2},{2,3},{3,4},{4,5},{5,6},{6,7},{8,9},{9,10},{10,11},{11... | collective-permute-start | bytes 7077896 | tf_op jit(solution)/shard_map/ppermute | solution.py:21
  72.5 2.8 %collective-permute-start = (f32[1,96,128]{1,2,0:T(8,128)S(1)}, f32[1,96,128]{1,2,0:T(8,128)S(1)}, u32[]{:S(2)}, u32[]{:S(2)}) collective-permute-start(f32[1,96,128]{1,2,0:T(8,128)S(1)} %get-tuple-element.50), channel_id=1, source_target_pairs={{0,1},{1,2},{2,3},{3,4},{4,5},{5,6},{6,7},{8,9},{9,10},{10,11},{11... | collective-permute-start | bytes 147464 | tf_op jit(solution)/shard_map/ppermute | solution.py:32
  73.8 4.8 %collective-permute-start.1 = (f32[1,96,128]{1,2,0:T(8,128)S(1)}, f32[1,96,128]{1,2,0:T(8,128)S(1)}, u32[]{:S(2)}, u32[]{:S(2)}) collective-permute-start(f32[1,96,128]{1,2,0:T(8,128)S(1)} %get-tuple-element.51), channel_id=1, source_target_pairs={{1,0},{2,1},{3,2},{4,3},{5,4},{6,5},{7,6},{9,8},{10,9},{11,10},{12... | collective-permute-start | bytes 147464 | tf_op jit(solution)/shard_map/ppermute | solution.py:34
  101.3 6.2 %collective-permute-start.3 = (f32[1,1,192,256]{3,2,1,0:T(8,128)S(1)}, f32[1,1,192,256]{3,2,1,0:T(8,128)S(1)}, u32[]{:S(2)}, u32[]{:S(2)}) collective-permute-start(f32[1,1,192,256]{3,2,1,0:T(8,128)S(1)} %get-tuple-element.36), channel_id=1, source_target_pairs={{0,1},{1,2},{2,3},{3,4},{4,5},{5,6},{6,7},{8,9},{9,10},{10,11},{11... | collective-permute-start | bytes 589832 | tf_op jit(solution)/shard_map/ppermute | solution.py:32
  106.2 3.3 %collective-permute-start.4 = (f32[1,1,192,256]{3,2,1,0:T(8,128)S(1)}, f32[1,1,192,256]{3,2,1,0:T(8,128)S(1)}, u32[]{:S(2)}, u32[]{:S(2)}) collective-permute-start(f32[1,1,192,256]{3,2,1,0:T(8,128)S(1)} %get-tuple-element.37), channel_id=1, source_target_pairs={{1,0},{2,1},{3,2},{4,3},{5,4},{6,5},{7,6},{9,8},{10,9},{11,10},{12... | collective-permute-start | bytes 589832 | tf_op jit(solution)/shard_map/ppermute | solution.py:34
  118.1 4.4 %copy-start.2 = (f32[12,192,256]{2,1,0:T(8,128)}, f32[12,192,256]{2,1,0:T(8,128)S(1)}, u32[]{:S(2)}) copy-start(f32[12,192,256]{2,1,0:T(8,128)S(1)} %get-tuple-element.26) | copy-start | bytes 7077892
  122.7 7.2 %collective-permute-start.6 = (f32[3,1,192,256]{3,2,1,0:T(8,128)S(1)}, f32[3,1,192,256]{3,2,1,0:T(8,128)S(1)}, u32[]{:S(2)}, u32[]{:S(2)}) collective-permute-start(f32[3,1,192,256]{3,2,1,0:T(8,128)S(1)} %get-tuple-element.29), channel_id=1, source_target_pairs={{0,1},{1,2},{2,3},{3,4},{4,5},{5,6},{6,7},{8,9},{9,10},{10,11},{11... | collective-permute-start | bytes 1769480 | tf_op jit(solution)/shard_map/ppermute | solution.py:32
  128.3 3.9 %collective-permute-start.5 = (f32[3,1,192,256]{3,2,1,0:T(8,128)S(1)}, f32[3,1,192,256]{3,2,1,0:T(8,128)S(1)}, u32[]{:S(2)}, u32[]{:S(2)}) collective-permute-start(f32[3,1,192,256]{3,2,1,0:T(8,128)S(1)} %get-tuple-element.30), channel_id=1, source_target_pairs={{1,0},{2,1},{3,2},{4,3},{5,4},{6,5},{7,6},{9,8},{10,9},{11,10},{12... | collective-permute-start | bytes 1769480 | tf_op jit(solution)/shard_map/ppermute | solution.py:34
  129.8 2.3 %copy-start.4 = (f32[3,1,192,256]{3,2,1,0:T(8,128)}, f32[3,1,192,256]{3,2,1,0:T(8,128)S(1)}, u32[]{:S(2)}) copy-start(f32[3,1,192,256]{3,2,1,0:T(8,128)S(1)} %collective-permute-done.6) | copy-start | bytes 1769476
  132.2 0.8 copy-start.5
  150.5 10.5 %collective-permute-start.7 = (f32[1,192,256]{2,1,0:T(8,128)S(1)}, f32[1,192,256]{2,1,0:T(8,128)S(1)}, u32[]{:S(2)}, u32[]{:S(2)}) collective-permute-start(f32[1,192,256]{2,1,0:T(8,128)S(1)} %get-tuple-element.34), channel_id=1, source_target_pairs={{0,1},{1,2},{2,3},{3,4},{4,5},{5,6},{6,7},{8,9},{9,10},{10,11},{11... | collective-permute-start | bytes 589832 | tf_op jit(solution)/shard_map/ppermute | solution.py:32
  159.7 3.3 %collective-permute-start.8 = (f32[1,192,256]{2,1,0:T(8,128)S(1)}, f32[1,192,256]{2,1,0:T(8,128)S(1)}, u32[]{:S(2)}, u32[]{:S(2)}) collective-permute-start(f32[1,192,256]{2,1,0:T(8,128)S(1)} %get-tuple-element.35), channel_id=1, source_target_pairs={{1,0},{2,1},{3,2},{4,3},{5,4},{6,5},{7,6},{9,8},{10,9},{11,10},{12... | collective-permute-start | bytes 589832 | tf_op jit(solution)/shard_map/ppermute | solution.py:34
  184.4 2.2 %copy-start.1 = (bf16[8,9,6912]{2,0,1:T(8,128)(2,1)S(1)}, bf16[8,9,6912]{2,0,1:T(8,128)(2,1)}, u32[]{:S(2)}) copy-start(bf16[8,9,6912]{2,0,1:T(8,128)(2,1)} %param.11) | copy-start | bytes 2985988
Sparse Core Ops, SparseCore 0:
  26.4 45.1 all-reduce.5
where the time goes:
time: 197 us; the launch traced here: 193 us
  waiting for transfers between devices  55.1 us (28%)
  other arithmetic  48.6 us (25%)
  local copies, waits for them, and re-layouts  36.1 us (18%)
  starting transfers between devices  30.4 us (15%)
  between operations  14.5 us (7%)
  matrix products  8.72 us (4%)
    psum x1, waiting for transfers between devices, body(): coarse = lax.psum(partial_density, 'band')[0]  45.3 us
    ppermute x4, starting transfers between devices, extended_2(): lax.ppermute(tail, axis, [(i, (i + 1) % count) for i in range(ends)])  21 us
    concatenate x3, other arithmetic, extended_2(): jnp.concatenate([lax.ppermute(tail, axis, [(i, (i + 1) % count) for i in...  14.8 us
    another operation x3, other arithmetic, transform(): jnp.stack([2.0 * by_sigma * grad_x, 2.0 * by_sigma * grad_y, 2.0 * by_sig...  10.5 us
    ppermute x4, waiting for transfers between devices, extended_2(): lax.ppermute(head, axis, [((i + 1) % count, i) for i in range(ends)])  9.73 us
    reshape x3, local copies, waits for them, and re-layouts, refine(): return joined.reshape(target)  8.89 us
    sub x1, other arithmetic, transform(): fine_potential = by_density - spread * half_inverse  7.04 us
    add x3, other arithmetic, restrict(): 0.125 * outer_low + 0.375 * (first_half + second_half) + 0.125 * outer_high  6.97 us
  transfers between devices with their start and end apart: 10, of which 6 were waited for; matrix products, arithmetic and copies ran while one was open for 11% of the time, Pallas kernels for 0%

commit v1 on v0

v1 whole, which is shorter than its diff:
```python
import functools

import jax
import jax.numpy as jnp
from jax import lax
from jax.experimental import pallas as pl
from jax.experimental.pallas import tpu as pltpu
from jax.sharding import PartitionSpec as P

SBX = 12
SBY = 24
SBZ = 24
GROUP = 384
LINES = 16
PAD = 32
HALO = 3

kappa_pbe = 0.804
mu_pbe = 0.2195
exchange_prefactor = -0.75 * (3.0 / 3.141592653589793) ** (1.0 / 3.0)
gradient_scale = 4.0 * (3.0 * 3.141592653589793**2) ** (2.0 / 3.0)
half_inverse = 0.5 / 0.2

f32 = jnp.float32
bf16 = jnp.bfloat16
MESH = pl.DeviceIdType.MESH


def iota(shape, dim):
    return lax.broadcasted_iota(jnp.int32, shape, dim)


def split(x):
    high = x.astype(bf16).astype(f32)
    return high, x - high


def weights(shape, terms):
    total = jnp.zeros(shape, f32)
    for mask, value in terms:
        total = jnp.where(mask, value, total)
    return total


def sources(fx):
    return (
        (0, 18, SBX, 0, 0, fx + HALO, 0),
        (0, 18, SBX, 0, -HALO, SBX - 1 + HALO, -1),
        (5760, 3, 2, 10, -HALO, 2, -2),
        (0, 5, 3, 0, fx, HALO, 1),
    )


def kernel(
    G, N, Q,
    part, mom, shp, off, cnt,
    out,
    win, recv, cext, v0, v1, v2, v3, offs, p0, p1, p2, p3, dens, flux, pot, zc,
    win_sem, ps_sem, pr_sem, cs_sem, cr_sem, vs_sem, vr_sem, os_sem, or_sem, gs_sem, gr_sem,
):
    _, cx, cy, cz = part.shape
    fx, fy, fz = 2 * cx, 2 * cy, 2 * cz
    yc = cy // Q
    yw = yc + 16
    fw = 2 * yc + 16
    j = lax.axis_index("band")
    d = lax.axis_index("dom")
    q = lax.rem(j, Q)

    def window_start(chunk):
        start = jnp.minimum(jnp.maximum(chunk * yc - 8, 0), cy - yw)
        return pl.multiple_of(start, 8)

    wstart = window_start(q)
    own = pltpu.make_async_copy(part.at[0, :, pl.ds(wstart, yw), :], win, win_sem)
    own.start()

    barrier = pltpu.get_barrier_semaphore()
    for k in range(1, G):
        pl.semaphore_signal(barrier, inc=1, device_id=(lax.rem(j + k, G), d), device_id_type=MESH)
    inside = {}
    for step in (-2, -1, 1, 2):
        inside[step] = jnp.logical_and(d + step >= 0, d + step < N)

        @pl.when(inside[step])
        def _(step=step):
            pl.semaphore_signal(barrier, inc=1, device_id=(j, d + step), device_id_type=MESH)

    count = G - 1
    for step in (-2, -1, 1, 2):
        count = count + jnp.where(inside[step], 1, 0)
    pl.semaphore_wait(barrier, count)

    part_copies = []
    for k in range(1, G):
        peer = lax.rem(j + k, G)
        copy = pltpu.make_async_remote_copy(
            src_ref=part.at[0, :, pl.ds(window_start(lax.rem(peer, Q)), yw), :],
            dst_ref=recv.at[k - 1],
            send_sem=ps_sem.at[k - 1],
            recv_sem=pr_sem.at[k - 1],
            device_id=(peer, d),
            device_id_type=MESH,
        )
        copy.start()
        part_copies.append(copy)

    slots = shp.shape[0]
    moments = mom[...].astype(f32)
    moments = jnp.where(iota(moments.shape, 1) < cnt[0], moments, 0.0)
    for s in range(slots):
        v0[s : s + 1, :] = jnp.sum(shp[s].astype(f32) * moments[:, s : s + 1], axis=0, keepdims=True)

    plan = sources(fx)
    blocks = (v0, v1, v2, v3)
    placed = (p0, p1, p2, p3)
    block_copies = [None]
    offset_copies = [None]
    for k in (1, 2, 3):
        lane, groups = plan[k][0], plan[k][1]
        step = -plan[k][6]
        block_copies.append(pltpu.make_async_remote_copy(
            src_ref=v0.at[:, pl.ds(lane, groups * GROUP)],
            dst_ref=blocks[k],
            send_sem=vs_sem.at[k], recv_sem=vr_sem.at[k],
            device_id=(j, d + step), device_id_type=MESH,
        ))
        offset_copies.append(pltpu.make_async_remote_copy(
            src_ref=off,
            dst_ref=offs.at[k],
            send_sem=os_sem.at[k], recv_sem=or_sem.at[k],
            device_id=(j, d + step), device_id_type=MESH,
        ))

        @pl.when(inside[step])
        def _(k=k):
            offset_copies[k].start()
            block_copies[k].start()

    line_mask = ((iota((LINES, GROUP), 1) * 2731) >> 16) == iota((LINES, GROUP), 0)
    k_rows = iota((GROUP, fz), 0)
    depth_in_line = iota((GROUP, fz), 1) - (k_rows - ((k_rows * 2731) >> 16) * SBZ)
    ystart = 2 * yc * q - 8

    def offset_of(k, row, s):
        return off[row, s] if k == 0 else offs[k, row, s]

    def unfold(k):
        _, groups, na, _, _, _, _ = plan[k]

        def one(s, carry):
            pick = jnp.where(depth_in_line == offset_of(k, 2, s), 1.0, 0.0).astype(bf16)
            pick = jnp.concatenate([pick, pick], axis=0)
            pieces = []
            for g in range(groups):
                line = blocks[k][pl.ds(s, 1), g * GROUP : (g + 1) * GROUP]
                high, low = split(line)
                wide = jnp.concatenate([
                    jnp.where(line_mask, jnp.broadcast_to(high, (LINES, GROUP)), 0.0),
                    jnp.where(line_mask, jnp.broadcast_to(low, (LINES, GROUP)), 0.0),
                ], axis=1)
                pieces.append(wide.astype(bf16))
            spread = jnp.dot(jnp.concatenate(pieces, axis=0), pick, preferred_element_type=f32)
            spread = spread[: na * SBY].reshape(na, SBY, fz)
            high, low = split(spread)
            gap = jnp.zeros((na, PAD - SBY, fz), f32)
            placed[k][s] = jnp.concatenate([high, gap, low, gap], axis=1).astype(bf16)
            return carry

        lax.fori_loop(0, slots, one, 0)

    def place(k, first):
        _, _, na, a0, x0, rows, slab = plan[k]
        width = slots * 2 * PAD
        lane = iota((1, width), 1)
        row_lane = jnp.zeros((1, width), jnp.int32)
        col_lane = jnp.zeros((1, width), jnp.int32)
        for s in range(slots):
            at = (lane >> 6) == s
            row_lane = jnp.where(at, offset_of(k, 0, s), row_lane)
            col_lane = jnp.where(at, offset_of(k, 1, s), col_lane)
        line = lane & (PAD - 1)
        target = jnp.where(line < SBY, col_lane + line, -1000)
        cols = jnp.where(iota((fw, width), 0) + ystart == target, 1.0, 0.0)

        def one(i, carry):
            x = x0 + i
            local = x - slab * fx - a0
            at = local - row_lane
            valid = jnp.logical_and(at >= 0, at < na)
            left = jnp.where(valid, cols, 0.0).astype(bf16)
            pieces = []
            for s in range(slots):
                index = jnp.clip(local - offset_of(k, 0, s), 0, na - 1)
                pieces.append(placed[k][s, index])
            right = jnp.concatenate(pieces, axis=0)
            value = jnp.dot(left, right, preferred_element_type=f32)
            if first:
                dens[x + HALO] = value
            else:
                dens[x + HALO] = dens[x + HALO] + value
            return carry

        lax.fori_loop(0, rows, one, 0)

    dens[0:HALO] = jnp.zeros((HALO, fw, fz), f32)
    unfold(0)
    place(0, True)

    own.wait()
    for copy in part_copies:
        copy.wait_recv()
    total = win[...]
    for k in range(1, G):
        total = total + recv[k - 1]
    cext[2 : cx + 2] = total
    rise = pltpu.make_async_remote_copy(
        src_ref=cext.at[pl.ds(cx, 2)], dst_ref=cext.at[pl.ds(0, 2)],
        send_sem=cs_sem.at[0], recv_sem=cr_sem.at[0],
        device_id=(j, d + 1), device_id_type=MESH,
    )
    sink = pltpu.make_async_remote_copy(
        src_ref=cext.at[pl.ds(2, 2)], dst_ref=cext.at[pl.ds(cx + 2, 2)],
        send_sem=cs_sem.at[1], recv_sem=cr_sem.at[1],
        device_id=(j, d - 1), device_id_type=MESH,
    )

    @pl.when(inside[1])
    def _():
        rise.start()

    @pl.when(inside[-1])
    def _():
        sink.start()

    for k in (3, 2, 1):

        @pl.when(inside[plan[k][6]])
        def _(k=k):
            offset_copies[k].wait_recv()
            block_copies[k].wait_recv()
            unfold(k)
            place(k, False)

    @pl.when(inside[-1])
    def _():
        rise.wait_recv()

    @pl.when(jnp.logical_not(inside[-1]))
    def _():
        cext[0:2] = jnp.zeros((2, yw, cz), f32)

    @pl.when(inside[1])
    def _():
        sink.wait_recv()

    @pl.when(jnp.logical_not(inside[1]))
    def _():
        cext[cx + 2 : cx + 4] = jnp.zeros((2, yw, cz), f32)

    rows = []
    for x in range(-HALO, fx + HALO):
        middle = (x >> 1) + 2
        other = middle + (1 if x % 2 else -1)
        rows.append(0.75 * cext[middle] + 0.25 * cext[other])
    count_x = fx + 2 * HALO
    stacked = jnp.concatenate(rows, axis=0)
    zi, zo = iota((cz, fz), 0), iota((cz, fz), 1)
    zm = zo >> 1
    zn = zm + ((zo & 1) << 1) - 1
    refine_z = weights((cz, fz), ((zi == zm, 0.75), (zi == zn, 0.25))).astype(bf16)
    refine_z = jnp.concatenate([refine_z, refine_z], axis=0)
    high, low = split(stacked)
    zc[...] = jnp.dot(
        jnp.concatenate([high, low], axis=1).astype(bf16), refine_z, preferred_element_type=f32
    ).reshape(count_x, yw, fz)
    yo = iota((fw, yw), 0) + ystart
    yi = iota((fw, yw), 1) + wstart
    ym = yo >> 1
    yn = ym + ((yo & 1) << 1) - 1
    grid = jnp.logical_and(yo >= 0, yo < fy)
    refine_y = weights(
        (fw, yw), ((jnp.logical_and(grid, yi == ym), 0.75), (jnp.logical_and(grid, yi == yn), 0.25))
    )
    refine_y = jnp.concatenate([refine_y, refine_y], axis=1).astype(bf16)

    def in_grid(x):
        g = d * fx + x
        return jnp.where(jnp.logical_and(g >= 0, g < N * fx), 1.0, 0.0).astype(f32)

    def refine_row(i, carry):
        high, low = split(zc[i])
        right = jnp.concatenate([high, low], axis=0).astype(bf16)
        value = jnp.dot(refine_y, right, preferred_element_type=f32)
        dens[i] = (dens[i] + value) * in_grid(i - HALO)
        return carry

    lax.fori_loop(0, count_x, refine_row, 0)

    lanes = iota((fw, fz), 1)
    first_lane, last_lane = lanes == 0, lanes == fz - 1

    def diff_z(f):
        after = jnp.where(last_lane, 0.0, pltpu.roll(f, fz - 1, 1))
        before = jnp.where(first_lane, 0.0, pltpu.roll(f, 1, 1))
        return (after - before) * half_inverse

    def diff_y(f):
        return (pltpu.roll(f, fw - 1, 0) - pltpu.roll(f, 1, 0)) * half_inverse

    def exchange_row(i, carry):
        n = dens[i + 1]
        gx = (dens[i + 2] - dens[i]) * half_inverse
        gy = diff_y(n)
        gz = diff_z(n)
        sigma = gx * gx + gy * gy + gz * gz
        live = n > 0.0
        log_n = jnp.log(jnp.where(live, n, 1.0))
        cube_root = jnp.exp(log_n * (1.0 / 3.0))
        inv_ft = jnp.exp(log_n * (-4.0 / 3.0))
        reduced = sigma * (inv_ft * inv_ft) * (1.0 / gradient_scale)
        inv_d = 1.0 / (1.0 + (mu_pbe / kappa_pbe) * reduced)
        slope = mu_pbe * inv_d * inv_d
        by_density = (exchange_prefactor * cube_root) * (
            (4.0 / 3.0) * (1.0 + kappa_pbe - kappa_pbe * inv_d) - (8.0 / 3.0) * reduced * slope
        )
        twice = jnp.where(live, (2.0 * exchange_prefactor / gradient_scale) * slope * inv_ft, 0.0)
        flux[i] = twice * gx
        pot[i] = by_density - (diff_y(twice * gy) + diff_z(twice * gz))
        return carry

    lax.fori_loop(0, fx + 4, exchange_row, 0)

    ro, ri = iota((yc, fw), 0), iota((yc, fw), 1)
    at = ri - 8 - 2 * ro
    grid = jnp.logical_and(ri + ystart >= 0, ri + ystart < fy)
    inner = jnp.logical_and(grid, jnp.logical_or(at == 0, at == 1))
    outer = jnp.logical_and(grid, jnp.logical_or(at == -1, at == 2))
    restrict_y = weights((yc, fw), ((inner, 0.375), (outer, 0.125)))
    restrict_y = jnp.concatenate([restrict_y, restrict_y], axis=1).astype(bf16)
    at = iota((fz, cz), 0) - 2 * iota((fz, cz), 1)
    inner = jnp.logical_or(at == 0, at == 1)
    outer = jnp.logical_or(at == -1, at == 2)
    restrict_z = weights((fz, cz), ((inner, 0.375), (outer, 0.125))).astype(bf16)
    restrict_z = jnp.concatenate([restrict_z, restrict_z], axis=0)

    def full(x):
        return (pot[x + 2] - (flux[x + 3] - flux[x + 1]) * half_inverse) * in_grid(x)

    ymine = pl.multiple_of(q * yc, 8)

    def restrict_row(i, carry):
        x = 2 * i
        mixed = 0.125 * (full(x - 1) + full(x + 2)) + 0.375 * (full(x) + full(x + 1))
        high, low = split(mixed)
        narrow = jnp.dot(
            restrict_y, jnp.concatenate([high, low], axis=0).astype(bf16), preferred_element_type=f32
        )
        high, low = split(narrow)
        out[i, pl.ds(ymine, yc), :] = jnp.dot(
            jnp.concatenate([high, low], axis=1).astype(bf16), restrict_z, preferred_element_type=f32
        )
        return carry

    lax.fori_loop(0, cx, restrict_row, 0)

    base = j - q
    gather = []
    for k in range(1, Q):
        copy = pltpu.make_async_remote_copy(
            src_ref=out.at[:, pl.ds(ymine, yc), :],
            dst_ref=out.at[:, pl.ds(ymine, yc), :],
            send_sem=gs_sem.at[k - 1], recv_sem=gr_sem.at[k - 1],
            device_id=(base + lax.rem(q + k, Q), d), device_id_type=MESH,
        )
        copy.start()
        gather.append(copy)
    for copy in part_copies:
        copy.wait_send()
    for k in (1, 2, 3):

        @pl.when(inside[-plan[k][6]])
        def _(k=k):
            offset_copies[k].wait_send()
            block_copies[k].wait_send()

    @pl.when(inside[1])
    def _():
        rise.wait_send()

    @pl.when(inside[-1])
    def _():
        sink.wait_send()

    for copy in gather:
        copy.wait()


def body(G, N, Q, partial_density, moments, shape_functions, sphere_offsets, owned_count):
    _, cx, cy, cz = partial_density.shape
    slots, _, block = shape_functions.shape
    fx, fz = 2 * cx, 2 * cz
    yc = cy // Q
    yw, fw = yc + 16, 2 * yc + 16
    plan = sources(fx)
    vmem = pl.BlockSpec(memory_space=pltpu.VMEM)
    smem = pl.BlockSpec(memory_space=pltpu.SMEM)
    return pl.pallas_call(
        functools.partial(kernel, G, N, Q),
        out_shape=jax.ShapeDtypeStruct((cx, cy, cz), f32),
        in_specs=[pl.BlockSpec(memory_space=pl.ANY), vmem, vmem, smem, smem],
        out_specs=vmem,
        scratch_shapes=[
            pltpu.VMEM((cx, yw, cz), f32),
            pltpu.VMEM((G - 1, cx, yw, cz), f32),
            pltpu.VMEM((cx + 4, yw, cz), f32),
        ]
        + [pltpu.VMEM((slots, p[1] * GROUP), f32) for p in plan]
        + [pltpu.SMEM((4,) + sphere_offsets.shape, jnp.int32)]
        + [pltpu.VMEM((slots, p[2], 2 * PAD, fz), bf16) for p in plan]
        + [
            pltpu.VMEM((fx + 2 * HALO, fw, fz), f32),
            pltpu.VMEM((fx + 4, fw, fz), f32),
            pltpu.VMEM((fx + 4, fw, fz), f32),
            pltpu.VMEM((fx + 2 * HALO, yw, fz), f32),
            pltpu.SemaphoreType.DMA(()),
            pltpu.SemaphoreType.DMA((G - 1,)),
            pltpu.SemaphoreType.DMA((G - 1,)),
            pltpu.SemaphoreType.DMA((2,)),
            pltpu.SemaphoreType.DMA((2,)),
            pltpu.SemaphoreType.DMA((4,)),
            pltpu.SemaphoreType.DMA((4,)),
            pltpu.SemaphoreType.DMA((4,)),
            pltpu.SemaphoreType.DMA((4,)),
            pltpu.SemaphoreType.DMA((Q - 1,)),
            pltpu.SemaphoreType.DMA((Q - 1,)),
        ],
        compiler_params=pltpu.CompilerParams(
            collective_id=0, has_side_effects=True, vmem_limit_bytes=48 * 1024 * 1024
        ),
    )(partial_density, moments, shape_functions, sphere_offsets, owned_count)


def solution(mesh):
    G, N = mesh.shape["band"], mesh.shape["dom"]

    def run(partial_density, *rest):
        cy = partial_density.shape[2]
        Q = max(c for c in range(1, G + 1) if G % c == 0 and cy % (8 * c) == 0)
        return jax.shard_map(
            functools.partial(body, G, N, Q),
            mesh=mesh,
            in_specs=(
                P("band", "dom", None, None),
                P(None, "dom"),
                P("dom", None, None),
                P(None, "dom"),
                P("dom"),
            ),
            out_specs=P("dom", None, None),
            check_vma=False,
        )(partial_density, *rest)

    return run
```

time: 197 us -> 37.4 us (0.19)
  the two profiles are of different devices: /device:TPU:0 before, /device:TPU:10 now
where the time goes in v1:
time: 37.4 us; the launch traced here: 37.2 us
  Pallas kernels  33.5 us (90%)
  local copies, waits for them, and re-layouts  2.93 us (8%)
  between operations  0.73 us (2%)
    pallas_call x1, Pallas kernels, body(): pl.pallas_call(functools.partial(kernel, G, N, Q), out_shape=jax.ShapeDty...  33.5 us
    unnamed x7, local copies, waits for them, and re-layouts  2.93 us

profile of v1, /device:TPU:10, one launch (start us, length us, event | category | flops | bytes accessed | tf_op | source)
XLA Modules:
  0.0 37.2 jit_solution(17338444087177807323)
XLA Ops:
  0.0 0.0 copy-start.1
  0.0 0.0 copy-start
  0.7 0.8 %copy.6.mom = bf16[9,8]{1,0:T(8,128)(2,1)S(1)} copy(bf16[9,8]{0,1:T(8,128)(2,1)} %param.6) | data formatting | bytes 288 | tf_op args[1]
  1.5 1.4 %copy.7.shp = bf16[8,9,6912]{2,1,0:T(8,128)(2,1)S(1)} copy(bf16[8,9,6912]{2,0,1:T(8,128)(2,1)} %param.7) | data formatting | bytes 1990656 | tf_op args[2]
  2.9 0.0 copy-done.1
  2.9 0.0 copy-done
  2.9 33.5 %shard_map.55 = f32[6,96,128]{2,1,0:T(8,128)S(1)} custom-call(f32[1,6,96,128]{3,2,1,0:T(8,128)S(1)} %copy-done, bf16[9,8]{1,0:T(8,128)(2,1)S(1)} %copy.6.mom, bf16[8,9,6912]{2,1,0:T(8,128)(2,1)S(1)} %copy.7.shp, s32[3,8]{1,0:T(4,128)S(1)} %copy-done.1, s32[1]{0:T(128)S(6)} %copy.9.cnt), custom_call_target="tpu_custom_call" | custom-call | tf_op jit(solution)/shard_map/pallas_call | solution.py:408
  36.5 0.7 %copy.10 = f32[6,96,128]{2,1,0:T(8,128)} copy(f32[6,96,128]{2,1,0:T(8,128)S(1)} %shard_map.55) | data formatting | bytes 589824
Async XLA Ops:
  0.0 2.9 %copy-start.1 = (s32[3,8]{1,0:T(4,128)S(1)}, s32[3,8]{1,0:T(4,128)}, u32[]{:S(2)}) copy-start(s32[3,8]{1,0:T(4,128)} %off.1) | copy-start | bytes 292
  0.0 2.9 %copy-start = (f32[1,6,96,128]{3,2,1,0:T(8,128)S(1)}, f32[1,6,96,128]{3,2,1,0:T(8,128)}, u32[]{:S(2)}) copy-start(f32[1,6,96,128]{3,2,1,0:T(8,128)} %part.1) | copy-start | bytes 884740

commit v2 on v1

--- a/solution.py
+++ b/solution.py
@@ -53,16 +53,16 @@
 
 def kernel(
     G, N, Q,
-    part, mom, shp, off, cnt,
+    part, mom, shp_hbm, off, cnt,
     out,
-    win, recv, cext, v0, v1, v2, v3, offs, p0, p1, p2, p3, dens, flux, pot, zc,
-    win_sem, ps_sem, pr_sem, cs_sem, cr_sem, vs_sem, vr_sem, os_sem, or_sem, gs_sem, gr_sem,
+    shp, win, recv, cext, v0, v1, v2, v3, vh, vl, offs, p0, p1, p2, p3, dens, flux, pot, zc,
+    shp_sem, win_sem, ps_sem, pr_sem, cs_sem, cr_sem, vs_sem, vr_sem, os_sem, or_sem, gs_sem, gr_sem,
 ):
     _, cx, cy, cz = part.shape
     fx, fy, fz = 2 * cx, 2 * cy, 2 * cz
     yc = cy // Q
     yw = yc + 16
-    fw = 2 * yc + 16
+    fw = 2 * yc + 8
     j = lax.axis_index("band")
     d = lax.axis_index("dom")
     q = lax.rem(j, Q)
@@ -74,6 +74,8 @@
     wstart = window_start(q)
     own = pltpu.make_async_copy(part.at[0, :, pl.ds(wstart, yw), :], win, win_sem)
     own.start()
+    fetch = pltpu.make_async_copy(shp_hbm, shp, shp_sem)
+    fetch.start()
 
     barrier = pltpu.get_barrier_semaphore()
     for k in range(1, G):
@@ -105,11 +107,17 @@
         copy.start()
         part_copies.append(copy)
 
-    slots = shp.shape[0]
+    channels, slots, _ = shp.shape
     moments = mom[...].astype(f32)
-    moments = jnp.where(iota(moments.shape, 1) < cnt[0], moments, 0.0)
-    for s in range(slots):
-        v0[s : s + 1, :] = jnp.sum(shp[s].astype(f32) * moments[:, s : s + 1], axis=0, keepdims=True)
+    moments = jnp.where(iota(moments.shape, 0) < cnt[0], moments, 0.0)
+    scales = [jnp.broadcast_to(moments[:, l : l + 1], (slots, GROUP)) for l in range(channels)]
+    fetch.wait()
+    for g in range(v0.shape[1] // GROUP):
+        at = slice(g * GROUP, (g + 1) * GROUP)
+        total = shp[0, :, at].astype(f32) * scales[0]
+        for l in range(1, channels):
+            total = total + shp[l, :, at].astype(f32) * scales[l]
+        v0[:, at] = total
 
     plan = sources(fx)
     blocks = (v0, v1, v2, v3)
@@ -140,21 +148,25 @@
     line_mask = ((iota((LINES, GROUP), 1) * 2731) >> 16) == iota((LINES, GROUP), 0)
     k_rows = iota((GROUP, fz), 0)
     depth_in_line = iota((GROUP, fz), 1) - (k_rows - ((k_rows * 2731) >> 16) * SBZ)
-    ystart = 2 * yc * q - 8
+    ystart = 2 * yc * q - 4
 
     def offset_of(k, row, s):
         return off[row, s] if k == 0 else offs[k, row, s]
 
     def unfold(k):
         _, groups, na, _, _, _, _ = plan[k]
+        width = groups * GROUP
+        high, low = split(blocks[k][...])
+        vh[:, :width] = high
+        vl[:, :width] = low
 
         def one(s, carry):
             pick = jnp.where(depth_in_line == offset_of(k, 2, s), 1.0, 0.0).astype(bf16)
             pick = jnp.concatenate([pick, pick], axis=0)
             pieces = []
             for g in range(groups):
-                line = blocks[k][pl.ds(s, 1), g * GROUP : (g + 1) * GROUP]
-                high, low = split(line)
+                high = vh[pl.ds(s, 1), g * GROUP : (g + 1) * GROUP]
+                low = vl[pl.ds(s, 1), g * GROUP : (g + 1) * GROUP]
                 wide = jnp.concatenate([
                     jnp.where(line_mask, jnp.broadcast_to(high, (LINES, GROUP)), 0.0),
                     jnp.where(line_mask, jnp.broadcast_to(low, (LINES, GROUP)), 0.0),
@@ -167,7 +179,7 @@
             placed[k][s] = jnp.concatenate([high, gap, low, gap], axis=1).astype(bf16)
             return carry
 
-        lax.fori_loop(0, slots, one, 0)
+        lax.fori_loop(0, slots, one, 0, unroll=2)
 
     def place(k, first):
         _, _, na, a0, x0, rows, slab = plan[k]
@@ -201,7 +213,7 @@
                 dens[x + HALO] = dens[x + HALO] + value
             return carry
 
-        lax.fori_loop(0, rows, one, 0)
+        lax.fori_loop(0, rows, one, 0, unroll=2 if rows % 2 == 0 else 3)
 
     dens[0:HALO] = jnp.zeros((HALO, fw, fz), f32)
     unfold(0)
@@ -295,7 +307,7 @@
         dens[i] = (dens[i] + value) * in_grid(i - HALO)
         return carry
 
-    lax.fori_loop(0, count_x, refine_row, 0)
+    lax.fori_loop(0, count_x, refine_row, 0, unroll=3)
 
     lanes = iota((fw, fz), 1)
     first_lane, last_lane = lanes == 0, lanes == fz - 1
@@ -329,10 +341,9 @@
         pot[i] = by_density - (diff_y(twice * gy) + diff_z(twice * gz))
         return carry
 
-    lax.fori_loop(0, fx + 4, exchange_row, 0)
 
     ro, ri = iota((yc, fw), 0), iota((yc, fw), 1)
-    at = ri - 8 - 2 * ro
+    at = ri - 4 - 2 * ro
     grid = jnp.logical_and(ri + ystart >= 0, ri + ystart < fy)
     inner = jnp.logical_and(grid, jnp.logical_or(at == 0, at == 1))
     outer = jnp.logical_and(grid, jnp.logical_or(at == -1, at == 2))
@@ -349,32 +360,41 @@
 
     ymine = pl.multiple_of(q * yc, 8)
 
-    def restrict_row(i, carry):
-        x = 2 * i
-        mixed = 0.125 * (full(x - 1) + full(x + 2)) + 0.375 * (full(x) + full(x + 1))
-        high, low = split(mixed)
-        narrow = jnp.dot(
-            restrict_y, jnp.concatenate([high, low], axis=0).astype(bf16), preferred_element_type=f32
-        )
-        high, low = split(narrow)
-        out[i, pl.ds(ymine, yc), :] = jnp.dot(
+    def restrict_rows(low_row, high_row):
+        pieces = []
+        for i in range(low_row, high_row):
+            x = 2 * i
+            mixed = 0.125 * (full(x - 1) + full(x + 2)) + 0.375 * (full(x) + full(x + 1))
+            high, low = split(mixed)
+            pieces.append(jnp.dot(
+                restrict_y,
+                jnp.concatenate([high, low], axis=0).astype(bf16),
+                preferred_element_type=f32,
+            ))
+        high, low = split(jnp.concatenate(pieces, axis=0))
+        result = jnp.dot(
             jnp.concatenate([high, low], axis=1).astype(bf16), restrict_z, preferred_element_type=f32
         )
-        return carry
-
-    lax.fori_loop(0, cx, restrict_row, 0)
+        out[low_row:high_row, pl.ds(ymine, yc), :] = result.reshape(high_row - low_row, yc, cz)
 
     base = j - q
+    half = cx // 2
     gather = []
-    for k in range(1, Q):
-        copy = pltpu.make_async_remote_copy(
-            src_ref=out.at[:, pl.ds(ymine, yc), :],
-            dst_ref=out.at[:, pl.ds(ymine, yc), :],
-            send_sem=gs_sem.at[k - 1], recv_sem=gr_sem.at[k - 1],
-            device_id=(base + lax.rem(q + k, Q), d), device_id_type=MESH,
-        )
-        copy.start()
-        gather.append(copy)
+    done = 0
+    for piece, (low_row, high_row) in enumerate(((0, half), (half, cx))):
+        lax.fori_loop(done, 2 * high_row + 4, exchange_row, 0)
+        done = 2 * high_row + 4
+        restrict_rows(low_row, high_row)
+        for k in range(1, Q):
+            at = (pl.ds(low_row, high_row - low_row), pl.ds(ymine, yc), slice(None))
+            copy = pltpu.make_async_remote_copy(
+                src_ref=out.at[at],
+                dst_ref=out.at[at],
+                send_sem=gs_sem.at[piece, k - 1], recv_sem=gr_sem.at[piece, k - 1],
+                device_id=(base + lax.rem(q + k, Q), d), device_id_type=MESH,
+            )
+            copy.start()
+            gather.append(copy)
     for copy in part_copies:
         copy.wait_send()
     for k in (1, 2, 3):
@@ -398,24 +418,27 @@
 
 def body(G, N, Q, partial_density, moments, shape_functions, sphere_offsets, owned_count):
     _, cx, cy, cz = partial_density.shape
-    slots, _, block = shape_functions.shape
+    slots, channels, block = shape_functions.shape
     fx, fz = 2 * cx, 2 * cz
     yc = cy // Q
-    yw, fw = yc + 16, 2 * yc + 16
+    yw, fw = yc + 16, 2 * yc + 8
     plan = sources(fx)
+    hbm = pl.BlockSpec(memory_space=pl.ANY)
     vmem = pl.BlockSpec(memory_space=pltpu.VMEM)
     smem = pl.BlockSpec(memory_space=pltpu.SMEM)
     return pl.pallas_call(
         functools.partial(kernel, G, N, Q),
         out_shape=jax.ShapeDtypeStruct((cx, cy, cz), f32),
-        in_specs=[pl.BlockSpec(memory_space=pl.ANY), vmem, vmem, smem, smem],
+        in_specs=[hbm, vmem, hbm, smem, smem],
         out_specs=vmem,
         scratch_shapes=[
+            pltpu.VMEM((channels, slots, block), bf16),
             pltpu.VMEM((cx, yw, cz), f32),
             pltpu.VMEM((G - 1, cx, yw, cz), f32),
             pltpu.VMEM((cx + 4, yw, cz), f32),
         ]
         + [pltpu.VMEM((slots, p[1] * GROUP), f32) for p in plan]
+        + [pltpu.VMEM((slots, block), f32)] * 2
         + [pltpu.SMEM((4,) + sphere_offsets.shape, jnp.int32)]
         + [pltpu.VMEM((slots, p[2], 2 * PAD, fz), bf16) for p in plan]
         + [
@@ -423,6 +446,7 @@
             pltpu.VMEM((fx + 4, fw, fz), f32),
             pltpu.VMEM((fx + 4, fw, fz), f32),
             pltpu.VMEM((fx + 2 * HALO, yw, fz), f32),
+            pltpu.SemaphoreType.DMA(()),
             pltpu.SemaphoreType.DMA(()),
             pltpu.SemaphoreType.DMA((G - 1,)),
             pltpu.SemaphoreType.DMA((G - 1,)),
@@ -432,13 +456,13 @@
             pltpu.SemaphoreType.DMA((4,)),
             pltpu.SemaphoreType.DMA((4,)),
             pltpu.SemaphoreType.DMA((4,)),
-            pltpu.SemaphoreType.DMA((Q - 1,)),
-            pltpu.SemaphoreType.DMA((Q - 1,)),
+            pltpu.SemaphoreType.DMA((2, Q - 1)),
+            pltpu.SemaphoreType.DMA((2, Q - 1)),
         ],
         compiler_params=pltpu.CompilerParams(
-            collective_id=0, has_side_effects=True, vmem_limit_bytes=48 * 1024 * 1024
+            collective_id=0, has_side_effects=True, vmem_limit_bytes=60 * 1024 * 1024
         ),
-    )(partial_density, moments, shape_functions, sphere_offsets, owned_count)
+    )(partial_density, moments.T, shape_functions.transpose(1, 0, 2), sphere_offsets, owned_count)
 
 
 def solution(mesh):

time: 37.4 us -> 29.7 us (0.79)
  the two profiles are of different devices: /device:TPU:10 before, /device:TPU:16 now
where the time goes in v2:
time: 29.7 us; the launch traced here: 29.5 us
  Pallas kernels  27.2 us (92%)
  local copies, waits for them, and re-layouts  1.69 us (6%)
  between operations  0.66 us (2%)
    pallas_call x1, Pallas kernels, body(): pl.pallas_call(functools.partial(kernel, G, N, Q), out_shape=jax.ShapeDty...  27.2 us
    unnamed x1, local copies, waits for them, and re-layouts  1.69 us

profile of v2, /device:TPU:16, one launch (start us, length us, event | category | flops | bytes accessed | tf_op | source)
XLA Modules:
  0.0 29.5 jit_solution(3710836337896323437)
XLA Ops:
  0.7 27.2 %shard_map.55 = f32[6,96,128]{2,1,0:T(8,128)} custom-call(f32[1,6,96,128]{3,2,1,0:T(8,128)} %part.1, bf16[8,9]{1,0:T(8,128)(2,1)} %bitcast.3, bf16[9,8,6912]{2,1,0:T(8,128)(2,1)} %bitcast.2, s32[3,8]{1,0:T(4,128)} %off.1, s32[1]{0:T(128)S(6)} %copy.7.cnt), custom_call_target="tpu_custom_call" | custom-call | tf_op jit(solution)/shard_map/pallas_call | solution.py:429
  27.8 1.7 %copy.8 = f32[6,96,128]{2,1,0:T(8,128)} copy(f32[6,96,128]{2,1,0:T(8,128)} %shard_map.55) | data formatting | bytes 589824

commit v3 on v2

--- a/solution.py
+++ b/solution.py
@@ -11,8 +11,9 @@
 SBY = 24
 SBZ = 24
 GROUP = 384
-LINES = 16
-PAD = 32
+LINES = 8
+SPAN = 256
+SLOT_LANES = 32
 HALO = 3
 
 kappa_pbe = 0.804
@@ -55,7 +56,7 @@
     G, N, Q,
     part, mom, shp_hbm, off, cnt,
     out,
-    shp, win, recv, cext, v0, v1, v2, v3, vh, vl, offs, p0, p1, p2, p3, dens, flux, pot, zc,
+    shp, win, recv, cext, v0, v1, v2, v3, vh, vl, offs, unfolder, wide, u0, u1, u2, u3, lined, lined_coarse, dens, flux, pot,
     shp_sem, win_sem, ps_sem, pr_sem, cs_sem, cr_sem, vs_sem, vr_sem, os_sem, or_sem, gs_sem, gr_sem,
 ):
     _, cx, cy, cz = part.shape
@@ -76,6 +77,14 @@
     own.start()
     fetch = pltpu.make_async_copy(shp_hbm, shp, shp_sem)
     fetch.start()
+
+    slots = shp.shape[1]
+    k_rows, k_lanes = iota((SPAN, SPAN), 0), iota((SPAN, SPAN), 1)
+    for h in range(2):
+        k_rows_h = k_rows + 128 * h
+        shift = k_lanes - (k_rows_h - ((k_rows_h * 2731) >> 16) * SBZ)
+        for s in range(slots):
+            unfolder[h, s] = jnp.where(shift == SLOT_LANES * s, 1.0, 0.0).astype(bf16)
 
     barrier = pltpu.get_barrier_semaphore()
     for k in range(1, G):
@@ -121,7 +130,7 @@
 
     plan = sources(fx)
     blocks = (v0, v1, v2, v3)
-    placed = (p0, p1, p2, p3)
+    folded = (u0, u1, u2, u3)
     block_copies = [None]
     offset_copies = [None]
     for k in (1, 2, 3):
@@ -145,78 +154,131 @@
             offset_copies[k].start()
             block_copies[k].start()
 
-    line_mask = ((iota((LINES, GROUP), 1) * 2731) >> 16) == iota((LINES, GROUP), 0)
-    k_rows = iota((GROUP, fz), 0)
-    depth_in_line = iota((GROUP, fz), 1) - (k_rows - ((k_rows * 2731) >> 16) * SBZ)
+    line_masks = []
+    for h in range(2):
+        lane = iota((LINES, SPAN), 1) + 128 * h
+        line_masks.append(((lane * 2731) >> 16) == iota((LINES, SPAN), 0) + LINES * h)
     ystart = 2 * yc * q - 4
 
     def offset_of(k, row, s):
         return off[row, s] if k == 0 else offs[k, row, s]
 
-    def unfold(k):
-        _, groups, na, _, _, _, _ = plan[k]
-        width = groups * GROUP
-        high, low = split(blocks[k][...])
-        vh[:, :width] = high
-        vl[:, :width] = low
+    def unfold(which):
+        starts = []
+        total = 0
+        for k in which:
+            starts.append(total)
+            width = plan[k][1] * GROUP
+            high, low = split(blocks[k][...])
+            vh[:, total : total + width] = high
+            vl[:, total : total + width] = low
+            total += width
+        groups = total // GROUP
 
         def one(s, carry):
-            pick = jnp.where(depth_in_line == offset_of(k, 2, s), 1.0, 0.0).astype(bf16)
-            pick = jnp.concatenate([pick, pick], axis=0)
-            pieces = []
-            for g in range(groups):
-                high = vh[pl.ds(s, 1), g * GROUP : (g + 1) * GROUP]
-                low = vl[pl.ds(s, 1), g * GROUP : (g + 1) * GROUP]
-                wide = jnp.concatenate([
-                    jnp.where(line_mask, jnp.broadcast_to(high, (LINES, GROUP)), 0.0),
-                    jnp.where(line_mask, jnp.broadcast_to(low, (LINES, GROUP)), 0.0),
-                ], axis=1)
-                pieces.append(wide.astype(bf16))
-            spread = jnp.dot(jnp.concatenate(pieces, axis=0), pick, preferred_element_type=f32)
-            spread = spread[: na * SBY].reshape(na, SBY, fz)
-            high, low = split(spread)
-            gap = jnp.zeros((na, PAD - SBY, fz), f32)
-            placed[k][s] = jnp.concatenate([high, gap, low, gap], axis=1).astype(bf16)
+            for h in range(2):
+                for t, source in enumerate((vh, vl)):
+                    pieces = []
+                    for g in range(groups):
+                        at = g * GROUP + 128 * h
+                        line = source[pl.ds(s, 1), at : at + SPAN]
+                        pieces.append(
+                            jnp.where(line_masks[h], jnp.broadcast_to(line, (LINES, SPAN)), 0.0)
+                        )
+                    lane = pl.multiple_of(s * (2 * SPAN) + t * SPAN, SPAN)
+                    wide[h, : groups * LINES, pl.ds(lane, SPAN)] = jnp.concatenate(
+                        pieces, axis=0
+                    ).astype(bf16)
             return carry
 
         lax.fori_loop(0, slots, one, 0, unroll=2)
+        halves = []
+        for h in range(2):
+            right = []
+            for s in range(slots):
+                right += [unfolder[h, s]] * 2
+            value = jnp.dot(
+                wide[h, : groups * LINES, :], jnp.concatenate(right, axis=0),
+                preferred_element_type=f32,
+            )
+            halves.append(value.reshape(groups, LINES, SPAN))
+        lines = jnp.stack(halves, axis=1).reshape(groups * 2 * LINES, SPAN)
+        for k, start in zip(which, starts):
+            na = plan[k][2]
+            at = start // GROUP * 2 * LINES
+            high, low = split(lines[at : at + na * SBY].reshape(na, SBY, SPAN))
+            folded[k][0:na] = jnp.concatenate([high, low], axis=1).astype(bf16)
+            folded[k][na] = jnp.zeros((2 * SBY, SPAN), bf16)
+
+    lane_tile = iota((16, 128), 1) >> 5
+    slot_masks = []
+    for s in range(4):
+        mask = jnp.where(lane_tile == s, 1.0, 0.0).astype(bf16)
+        slot_masks.append(jnp.concatenate([mask] * 3, axis=0))
 
     def place(k, first):
         _, _, na, a0, x0, rows, slab = plan[k]
-        width = slots * 2 * PAD
+        rows += rows % 2
+        width = 4 * 2 * SBY
         lane = iota((1, width), 1)
-        row_lane = jnp.zeros((1, width), jnp.int32)
-        col_lane = jnp.zeros((1, width), jnp.int32)
+        in_slot = (lane * 1366) >> 16
+        b = lane - ((lane * 2731) >> 16) * SBY
+        picks = []
+        for h in range(2):
+            target = b
+            for s in range(4):
+                target = target + jnp.where(in_slot == s, offset_of(k, 1, 4 * h + s), 0)
+            picks.append(
+                jnp.where(iota((fw, width), 0) + ystart == target, 1.0, 0.0).astype(bf16)
+            )
+
+        def one(i, carry):
+            halves = []
+            for h in range(2):
+                columns = []
+                for step in range(2):
+                    local = x0 + 2 * i + step - slab * fx - a0
+                    pieces = []
+                    for s in range(4):
+                        at = local - offset_of(k, 0, 4 * h + s)
+                        at = jnp.where(jnp.logical_and(at >= 0, at < na), at, na)
+                        pieces.append(folded[k][at, :, 128 * h : 128 * h + 128] * slot_masks[s])
+                    columns.append(jnp.concatenate(pieces, axis=0))
+                halves.append(jnp.dot(
+                    picks[h], jnp.concatenate(columns, axis=1), preferred_element_type=f32
+                ))
+            parts = []
+            for step in range(2):
+                at = slice(128 * step, 128 * step + 128)
+                value = jnp.concatenate([halves[0][:, at], halves[1][:, at]], axis=1)
+                parts.append(jnp.concatenate(split(value), axis=1))
+            lined[pl.ds(pl.multiple_of(i * (2 * fw), 2 * fw), 2 * fw), :] = jnp.concatenate(
+                parts, axis=0
+            ).astype(bf16)
+            return carry
+
+        lax.fori_loop(0, rows // 2, one, 0, unroll=2 if rows % 4 == 0 else 1)
+        lane_row = iota((SPAN, fz), 0)
+        depth = lane_row & (SLOT_LANES - 1)
         for s in range(slots):
-            at = (lane >> 6) == s
-            row_lane = jnp.where(at, offset_of(k, 0, s), row_lane)
-            col_lane = jnp.where(at, offset_of(k, 1, s), col_lane)
-        line = lane & (PAD - 1)
-        target = jnp.where(line < SBY, col_lane + line, -1000)
-        cols = jnp.where(iota((fw, width), 0) + ystart == target, 1.0, 0.0)
-
-        def one(i, carry):
-            x = x0 + i
-            local = x - slab * fx - a0
-            at = local - row_lane
-            valid = jnp.logical_and(at >= 0, at < na)
-            left = jnp.where(valid, cols, 0.0).astype(bf16)
-            pieces = []
-            for s in range(slots):
-                index = jnp.clip(local - offset_of(k, 0, s), 0, na - 1)
-                pieces.append(placed[k][s, index])
-            right = jnp.concatenate(pieces, axis=0)
-            value = jnp.dot(left, right, preferred_element_type=f32)
+            depth = depth + jnp.where((lane_row >> 5) == s, offset_of(k, 2, s), 0)
+        inside_line = (lane_row & (SLOT_LANES - 1)) < SBZ
+        hit = jnp.logical_and(inside_line, iota((SPAN, fz), 1) == depth)
+        pick = jnp.where(hit, 1.0, 0.0).astype(bf16)
+        pick = jnp.concatenate([pick, pick], axis=0)
+        for start in range(0, rows, 4):
+            size = min(4, rows - start)
+            value = jnp.dot(
+                lined[start * fw : (start + size) * fw, :], pick, preferred_element_type=f32
+            ).reshape(size, fw, fz)
+            at = x0 + HALO + start
             if first:
-                dens[x + HALO] = value
+                dens[at : at + size] = value
             else:
-                dens[x + HALO] = dens[x + HALO] + value
-            return carry
-
-        lax.fori_loop(0, rows, one, 0, unroll=2 if rows % 2 == 0 else 3)
+                dens[at : at + size] = dens[at : at + size] + value
 
     dens[0:HALO] = jnp.zeros((HALO, fw, fz), f32)
-    unfold(0)
+    unfold((0,))
     place(0, True)
 
     own.wait()
@@ -245,14 +307,23 @@
     def _():
         sink.start()
 
-    for k in (3, 2, 1):
+    for k in (1, 2, 3):
 
         @pl.when(inside[plan[k][6]])
         def _(k=k):
             offset_copies[k].wait_recv()
             block_copies[k].wait_recv()
-            unfold(k)
-            place(k, False)
+
+        @pl.when(jnp.logical_not(inside[plan[k][6]]))
+        def _(k=k):
+            blocks[k][...] = jnp.zeros(blocks[k].shape, f32)
+            for row in range(3):
+                for s in range(slots):
+                    offs[k, row, s] = 0
+
+    unfold((1, 2, 3))
+    for k in (1, 2, 3):
+        place(k, False)
 
     @pl.when(inside[-1])
     def _():
@@ -270,22 +341,12 @@
     def _():
         cext[cx + 2 : cx + 4] = jnp.zeros((2, yw, cz), f32)
 
-    rows = []
-    for x in range(-HALO, fx + HALO):
-        middle = (x >> 1) + 2
-        other = middle + (1 if x % 2 else -1)
-        rows.append(0.75 * cext[middle] + 0.25 * cext[other])
     count_x = fx + 2 * HALO
-    stacked = jnp.concatenate(rows, axis=0)
     zi, zo = iota((cz, fz), 0), iota((cz, fz), 1)
     zm = zo >> 1
     zn = zm + ((zo & 1) << 1) - 1
     refine_z = weights((cz, fz), ((zi == zm, 0.75), (zi == zn, 0.25))).astype(bf16)
     refine_z = jnp.concatenate([refine_z, refine_z], axis=0)
-    high, low = split(stacked)
-    zc[...] = jnp.dot(
-        jnp.concatenate([high, low], axis=1).astype(bf16), refine_z, preferred_element_type=f32
-    ).reshape(count_x, yw, fz)
     yo = iota((fw, yw), 0) + ystart
     yi = iota((fw, yw), 1) + wstart
     ym = yo >> 1
@@ -300,14 +361,26 @@
         g = d * fx + x
         return jnp.where(jnp.logical_and(g >= 0, g < N * fx), 1.0, 0.0).astype(f32)
 
-    def refine_row(i, carry):
-        high, low = split(zc[i])
-        right = jnp.concatenate([high, low], axis=0).astype(bf16)
+    def refine_pair(i, carry):
+        low_cell, high_cell = cext[i], cext[i + 1]
+        odd = 0.75 * low_cell + 0.25 * high_cell
+        even = 0.75 * high_cell + 0.25 * low_cell
+        both = jnp.concatenate([odd, even], axis=1)
+        right = jnp.concatenate(split(both), axis=0).astype(bf16)
         value = jnp.dot(refine_y, right, preferred_element_type=f32)
-        dens[i] = (dens[i] + value) * in_grid(i - HALO)
+        value = jnp.concatenate([value[:, :cz], value[:, cz:]], axis=0)
+        lined_coarse[pl.ds(pl.multiple_of(i * (2 * fw), 2 * fw), 2 * fw), :] = jnp.concatenate(
+            split(value), axis=1
+        ).astype(bf16)
         return carry
 
-    lax.fori_loop(0, count_x, refine_row, 0, unroll=3)
+    lax.fori_loop(0, count_x // 2, refine_pair, 0, unroll=3)
+    for start in range(0, count_x, 3):
+        value = jnp.dot(
+            lined_coarse[start * fw : (start + 3) * fw, :], refine_z, preferred_element_type=f32
+        ).reshape(3, fw, fz)
+        for i in range(3):
+            dens[start + i] = (dens[start + i] + value[i]) * in_grid(start + i - HALO)
 
     lanes = iota((fw, fz), 1)
     first_lane, last_lane = lanes == 0, lanes == fz - 1
@@ -315,14 +388,14 @@
     def diff_z(f):
         after = jnp.where(last_lane, 0.0, pltpu.roll(f, fz - 1, 1))
         before = jnp.where(first_lane, 0.0, pltpu.roll(f, 1, 1))
-        return (after - before) * half_inverse
+        return after - before
 
     def diff_y(f):
-        return (pltpu.roll(f, fw - 1, 0) - pltpu.roll(f, 1, 0)) * half_inverse
+        return pltpu.roll(f, fw - 1, 0) - pltpu.roll(f, 1, 0)
 
     def exchange_row(i, carry):
         n = dens[i + 1]
-        gx = (dens[i + 2] - dens[i]) * half_inverse
+        gx = dens[i + 2] - dens[i]
         gy = diff_y(n)
         gz = diff_z(n)
         sigma = gx * gx + gy * gy + gz * gz
@@ -330,13 +403,13 @@
         log_n = jnp.log(jnp.where(live, n, 1.0))
         cube_root = jnp.exp(log_n * (1.0 / 3.0))
         inv_ft = jnp.exp(log_n * (-4.0 / 3.0))
-        reduced = sigma * (inv_ft * inv_ft) * (1.0 / gradient_scale)
+        reduced = sigma * (inv_ft * inv_ft) * (half_inverse * half_inverse / gradient_scale)
         inv_d = 1.0 / (1.0 + (mu_pbe / kappa_pbe) * reduced)
         slope = mu_pbe * inv_d * inv_d
         by_density = (exchange_prefactor * cube_root) * (
             (4.0 / 3.0) * (1.0 + kappa_pbe - kappa_pbe * inv_d) - (8.0 / 3.0) * reduced * slope
         )
-        twice = jnp.where(live, (2.0 * exchange_prefactor / gradient_scale) * slope * inv_ft, 0.0)
+        twice = jnp.where(live, (2.0 * exchange_prefactor * half_inverse * half_inverse / gradient_scale) * slope * inv_ft, 0.0)
         flux[i] = twice * gx
         pot[i] = by_density - (diff_y(twice * gy) + diff_z(twice * gz))
         return carry
@@ -356,7 +429,7 @@
     restrict_z = jnp.concatenate([restrict_z, restrict_z], axis=0)
 
     def full(x):
-        return (pot[x + 2] - (flux[x + 3] - flux[x + 1]) * half_inverse) * in_grid(x)
+        return (pot[x + 2] - (flux[x + 3] - flux[x + 1])) * in_grid(x)
 
     ymine = pl.multiple_of(q * yc, 8)
 
@@ -423,7 +496,7 @@
     yc = cy // Q
     yw, fw = yc + 16, 2 * yc + 8
     plan = sources(fx)
-    hbm = pl.BlockSpec(memory_space=pl.ANY)
+    hbm = pl.BlockSpec(memory_space=pltpu.HBM)
     vmem = pl.BlockSpec(memory_space=pltpu.VMEM)
     smem = pl.BlockSpec(memory_space=pltpu.SMEM)
     return pl.pallas_call(
@@ -438,14 +511,16 @@
             pltpu.VMEM((cx + 4, yw, cz), f32),
         ]
         + [pltpu.VMEM((slots, p[1] * GROUP), f32) for p in plan]
-        + [pltpu.VMEM((slots, block), f32)] * 2
+        + [pltpu.VMEM((slots, 26 * GROUP), f32)] * 2
         + [pltpu.SMEM((4,) + sphere_offsets.shape, jnp.int32)]
-        + [pltpu.VMEM((slots, p[2], 2 * PAD, fz), bf16) for p in plan]
+        + [pltpu.VMEM((2, slots, SPAN, SPAN), bf16), pltpu.VMEM((2, 26 * LINES, slots * 2 * SPAN), bf16)]
+        + [pltpu.VMEM((p[2] + 1, 2 * SBY, SPAN), bf16) for p in plan]
         + [
-            pltpu.VMEM((fx + 2 * HALO, fw, fz), f32),
+            pltpu.VMEM(((fx + 4) * fw, 2 * SPAN), bf16),
+            pltpu.VMEM(((fx + 2 * HALO) * fw, 2 * cz), bf16),
+            pltpu.VMEM((fx + 2 * HALO + 1, fw, fz), f32),
             pltpu.VMEM((fx + 4, fw, fz), f32),
             pltpu.VMEM((fx + 4, fw, fz), f32),
-            pltpu.VMEM((fx + 2 * HALO, yw, fz), f32),
             pltpu.SemaphoreType.DMA(()),
             pltpu.SemaphoreType.DMA(()),
             pltpu.SemaphoreType.DMA((G - 1,)),
@@ -460,7 +535,7 @@
             pltpu.SemaphoreType.DMA((2, Q - 1)),
         ],
         compiler_params=pltpu.CompilerParams(
-            collective_id=0, has_side_effects=True, vmem_limit_bytes=60 * 1024 * 1024
+            collective_id=0, has_side_effects=True, vmem_limit_bytes=40 * 1024 * 1024
         ),
     )(partial_density, moments.T, shape_functions.transpose(1, 0, 2), sphere_offsets, owned_count)
 

time: 29.7 us -> 30 us (1.010)
  the two profiles are of different devices: /device:TPU:16 before, /device:TPU:0 now
where the time goes in v3:
time: 30 us; the launch traced here: 29.7 us
  Pallas kernels  25.5 us (85%)
  local copies, waits for them, and re-layouts  3.55 us (12%)
  between operations  0.69 us (2%)
    pallas_call x1, Pallas kernels, body(): pl.pallas_call(functools.partial(kernel, G, N, Q), out_shape=jax.ShapeDty...  25.5 us
    unnamed x9, local copies, waits for them, and re-layouts  3.55 us

profile of v3, /device:TPU:0, one launch (start us, length us, event | category | flops | bytes accessed | tf_op | source)
XLA Modules:
  0.0 29.7 jit_solution(15694618556317186051)
XLA Ops:
  0.0 0.0 copy-start.3
  0.7 0.0 copy-start.2
  0.7 0.0 copy-done.3
  0.7 0.7 %copy-done.2 = bf16[9,8]{0,1:T(8,128)(2,1)S(1)} copy-done((bf16[9,8]{0,1:T(8,128)(2,1)S(1)}, bf16[9,8]{0,1:T(8,128)(2,1)}, u32[]{:S(2)}) %copy-start.2) | copy-done | bytes 168
  1.4 0.0 copy-start
  1.4 1.2 %copy-done = bf16[8,9,6912]{2,0,1:T(8,128)(2,1)S(1)} copy-done((bf16[8,9,6912]{2,0,1:T(8,128)(2,1)S(1)}, bf16[8,9,6912]{2,0,1:T(8,128)(2,1)}, u32[]{:S(2)}) %copy-start) | copy-done | bytes 995352
  2.6 0.0 copy-start.1
  2.6 1.0 %copy-done.1 = f32[1,6,96,128]{3,2,1,0:T(8,128)S(1)} copy-done((f32[1,6,96,128]{3,2,1,0:T(8,128)S(1)}, f32[1,6,96,128]{3,2,1,0:T(8,128)}, u32[]{:S(2)}) %copy-start.1) | copy-done | bytes 294936
  3.5 25.5 %shard_map.55 = f32[6,96,128]{2,1,0:T(8,128)S(1)} custom-call(f32[1,6,96,128]{3,2,1,0:T(8,128)S(1)} %copy-done.1, bf16[8,9]{1,0:T(8,128)(2,1)S(1)} %bitcast.3, bf16[9,8,6912]{2,1,0:T(8,128)(2,1)S(1)} %bitcast.2, s32[3,8]{1,0:T(4,128)S(1)} %copy-done.3, s32[1]{0:T(128)S(6)} %copy.7.cnt), custom_call_target="tpu_custom_call" | custom-call | tf_op jit(solution)/shard_map/pallas_call | solution.py:502
  29.0 0.7 %copy.8 = f32[6,96,128]{2,1,0:T(8,128)} copy(f32[6,96,128]{2,1,0:T(8,128)S(1)} %shard_map.55) | data formatting | bytes 589824
Async XLA Ops:
  0.0 0.7 %copy-start.3 = (s32[3,8]{1,0:T(4,128)S(1)}, s32[3,8]{1,0:T(4,128)}, u32[]{:S(2)}) copy-start(s32[3,8]{1,0:T(4,128)} %off.1) | copy-start | bytes 292
  0.7 0.7 %copy-start.2 = (bf16[9,8]{0,1:T(8,128)(2,1)S(1)}, bf16[9,8]{0,1:T(8,128)(2,1)}, u32[]{:S(2)}) copy-start(bf16[9,8]{0,1:T(8,128)(2,1)} %param.6) | copy-start | bytes 436
  1.4 1.2 %copy-start = (bf16[8,9,6912]{2,0,1:T(8,128)(2,1)S(1)}, bf16[8,9,6912]{2,0,1:T(8,128)(2,1)}, u32[]{:S(2)}) copy-start(bf16[8,9,6912]{2,0,1:T(8,128)(2,1)} %param.7) | copy-start | bytes 2985988
  2.6 1.0 %copy-start.1 = (f32[1,6,96,128]{3,2,1,0:T(8,128)S(1)}, f32[1,6,96,128]{3,2,1,0:T(8,128)}, u32[]{:S(2)}) copy-start(f32[1,6,96,128]{3,2,1,0:T(8,128)} %part.1) | copy-start | bytes 884740

commit v4 on v3

--- a/solution.py
+++ b/solution.py
@@ -56,8 +56,8 @@
     G, N, Q,
     part, mom, shp_hbm, off, cnt,
     out,
-    shp, win, recv, cext, v0, v1, v2, v3, vh, vl, offs, unfolder, wide, u0, u1, u2, u3, lined, lined_coarse, dens, flux, pot,
-    shp_sem, win_sem, ps_sem, pr_sem, cs_sem, cr_sem, vs_sem, vr_sem, os_sem, or_sem, gs_sem, gr_sem,
+    shp, win, recv, cext, v0, v1, v2, v3, vh, vl, offs, unfolder, wide, u0, u1, u2, u3, lined, lined_coarse, dens, flux, pot, mine,
+    shp_sem, win_sem, ps_sem, pr_sem, cs_sem, cr_sem, vs_sem, vr_sem, os_sem, or_sem, gs_sem, gr_sem, keep_sem,
 ):
     _, cx, cy, cz = part.shape
     fx, fy, fz = 2 * cx, 2 * cy, 2 * cz
@@ -68,23 +68,17 @@
     d = lax.axis_index("dom")
     q = lax.rem(j, Q)
 
-    def window_start(chunk):
-        start = jnp.minimum(jnp.maximum(chunk * yc - 8, 0), cy - yw)
-        return pl.multiple_of(start, 8)
-
-    wstart = window_start(q)
-    own = pltpu.make_async_copy(part.at[0, :, pl.ds(wstart, yw), :], win, win_sem)
+    def chunk_of(index):
+        return pl.ds(pl.multiple_of(lax.rem(index, Q) * yc, 8), yc)
+
+    own = pltpu.make_async_copy(part.at[0, :, chunk_of(j), :], win, win_sem)
     own.start()
     fetch = pltpu.make_async_copy(shp_hbm, shp, shp_sem)
     fetch.start()
-
+    cext[...] = jnp.zeros(cext.shape, f32)
+    base = j - q
+    ystart = 2 * yc * q - 4
     slots = shp.shape[1]
-    k_rows, k_lanes = iota((SPAN, SPAN), 0), iota((SPAN, SPAN), 1)
-    for h in range(2):
-        k_rows_h = k_rows + 128 * h
-        shift = k_lanes - (k_rows_h - ((k_rows_h * 2731) >> 16) * SBZ)
-        for s in range(slots):
-            unfolder[h, s] = jnp.where(shift == SLOT_LANES * s, 1.0, 0.0).astype(bf16)
 
     barrier = pltpu.get_barrier_semaphore()
     for k in range(1, G):
@@ -97,16 +91,31 @@
         def _(step=step):
             pl.semaphore_signal(barrier, inc=1, device_id=(j, d + step), device_id_type=MESH)
 
+    sides = [(dj, dd) for dj in (-1, 0, 1) for dd in (-1, 0, 1) if dj or dd]
+    beside = {}
+    for dj, dd in sides:
+        there = jnp.logical_and(q + dj >= 0, q + dj < Q)
+        if dd:
+            there = jnp.logical_and(there, inside[dd])
+        beside[dj, dd] = there
+        if dj and dd:
+
+            @pl.when(there)
+            def _(dj=dj, dd=dd):
+                pl.semaphore_signal(barrier, inc=1, device_id=(j + dj, d + dd), device_id_type=MESH)
+
     count = G - 1
-    for step in (-2, -1, 1, 2):
-        count = count + jnp.where(inside[step], 1, 0)
+    for there in [inside[step] for step in (-2, -1, 1, 2)] + [
+        beside[dj, dd] for dj, dd in sides if dj and dd
+    ]:
+        count = count + jnp.where(there, 1, 0)
     pl.semaphore_wait(barrier, count)
 
     part_copies = []
     for k in range(1, G):
         peer = lax.rem(j + k, G)
         copy = pltpu.make_async_remote_copy(
-            src_ref=part.at[0, :, pl.ds(window_start(lax.rem(peer, Q)), yw), :],
+            src_ref=part.at[0, :, chunk_of(peer), :],
             dst_ref=recv.at[k - 1],
             send_sem=ps_sem.at[k - 1],
             recv_sem=pr_sem.at[k - 1],
@@ -116,7 +125,7 @@
         copy.start()
         part_copies.append(copy)
 
-    channels, slots, _ = shp.shape
+    channels = shp.shape[0]
     moments = mom[...].astype(f32)
     moments = jnp.where(iota(moments.shape, 0) < cnt[0], moments, 0.0)
     scales = [jnp.broadcast_to(moments[:, l : l + 1], (slots, GROUP)) for l in range(channels)]
@@ -158,7 +167,12 @@
     for h in range(2):
         lane = iota((LINES, SPAN), 1) + 128 * h
         line_masks.append(((lane * 2731) >> 16) == iota((LINES, SPAN), 0) + LINES * h)
-    ystart = 2 * yc * q - 4
+    k_rows, k_lanes = iota((SPAN, 128), 0), iota((SPAN, 128), 1)
+    for h in range(2):
+        k_rows_h = k_rows + 128 * h
+        shift = k_lanes - (k_rows_h - ((k_rows_h * 2731) >> 16) * SBZ)
+        for s in range(4):
+            unfolder[h, s] = jnp.where(shift == SLOT_LANES * s, 1.0, 0.0).astype(bf16)
 
     def offset_of(k, row, s):
         return off[row, s] if k == 0 else offs[k, row, s]
@@ -195,12 +209,17 @@
         halves = []
         for h in range(2):
             right = []
-            for s in range(slots):
+            for s in range(4):
                 right += [unfolder[h, s]] * 2
-            value = jnp.dot(
-                wide[h, : groups * LINES, :], jnp.concatenate(right, axis=0),
-                preferred_element_type=f32,
-            )
+            right = jnp.concatenate(right, axis=0)
+            value = [
+                jnp.dot(
+                    wide[h, : groups * LINES, t * 8 * SPAN : (t + 1) * 8 * SPAN], right,
+                    preferred_element_type=f32,
+                )
+                for t in range(2)
+            ]
+            value = jnp.concatenate(value, axis=1)
             halves.append(value.reshape(groups, LINES, SPAN))
         lines = jnp.stack(halves, axis=1).reshape(groups * 2 * LINES, SPAN)
         for k, start in zip(which, starts):
@@ -281,65 +300,54 @@
     unfold((0,))
     place(0, True)
 
+    for k in (1, 2, 3):
+
+        @pl.when(inside[plan[k][6]])
+        def _(k=k):
+            offset_copies[k].wait_recv()
+            block_copies[k].wait_recv()
+
+        @pl.when(jnp.logical_not(inside[plan[k][6]]))
+        def _(k=k):
+            blocks[k][...] = jnp.zeros(blocks[k].shape, f32)
+            for row in range(3):
+                for s in range(slots):
+                    offs[k, row, s] = 0
+
+    unfold((1, 2, 3))
+
     own.wait()
     for copy in part_copies:
         copy.wait_recv()
     total = win[...]
     for k in range(1, G):
         total = total + recv[k - 1]
-    cext[2 : cx + 2] = total
-    rise = pltpu.make_async_remote_copy(
-        src_ref=cext.at[pl.ds(cx, 2)], dst_ref=cext.at[pl.ds(0, 2)],
-        send_sem=cs_sem.at[0], recv_sem=cr_sem.at[0],
-        device_id=(j, d + 1), device_id_type=MESH,
-    )
-    sink = pltpu.make_async_remote_copy(
-        src_ref=cext.at[pl.ds(2, 2)], dst_ref=cext.at[pl.ds(cx + 2, 2)],
-        send_sem=cs_sem.at[1], recv_sem=cr_sem.at[1],
-        device_id=(j, d - 1), device_id_type=MESH,
-    )
-
-    @pl.when(inside[1])
-    def _():
-        rise.start()
-
-    @pl.when(inside[-1])
-    def _():
-        sink.start()
-
-    for k in (1, 2, 3):
-
-        @pl.when(inside[plan[k][6]])
-        def _(k=k):
-            offset_copies[k].wait_recv()
-            block_copies[k].wait_recv()
-
-        @pl.when(jnp.logical_not(inside[plan[k][6]]))
-        def _(k=k):
-            blocks[k][...] = jnp.zeros(blocks[k].shape, f32)
-            for row in range(3):
-                for s in range(slots):
-                    offs[k, row, s] = 0
-
-    unfold((1, 2, 3))
+    cext[2 : cx + 2, 8 : 8 + yc] = total
+    rows_from = {-1: pl.ds(2, 2), 0: pl.ds(2, cx), 1: pl.ds(cx, 2)}
+    rows_to = {-1: pl.ds(cx + 2, 2), 0: pl.ds(2, cx), 1: pl.ds(0, 2)}
+    cols_from = {-1: pl.ds(8, 8), 0: pl.ds(8, yc), 1: pl.ds(yc, 8)}
+    cols_to = {-1: pl.ds(yc + 8, 8), 0: pl.ds(8, yc), 1: pl.ds(0, 8)}
+    halo_copies = {}
+    for n, (dj, dd) in enumerate(sides):
+        halo_copies[dj, dd] = pltpu.make_async_remote_copy(
+            src_ref=cext.at[rows_from[dd], cols_from[dj]],
+            dst_ref=cext.at[rows_to[dd], cols_to[dj]],
+            send_sem=cs_sem.at[n], recv_sem=cr_sem.at[n],
+            device_id=(j + dj, d + dd), device_id_type=MESH,
+        )
+
+        @pl.when(beside[dj, dd])
+        def _(dj=dj, dd=dd):
+            halo_copies[dj, dd].start()
+
     for k in (1, 2, 3):
         place(k, False)
 
-    @pl.when(inside[-1])
-    def _():
-        rise.wait_recv()
-
-    @pl.when(jnp.logical_not(inside[-1]))
-    def _():
-        cext[0:2] = jnp.zeros((2, yw, cz), f32)
-
-    @pl.when(inside[1])
-    def _():
-        sink.wait_recv()
-
-    @pl.when(jnp.logical_not(inside[1]))
-    def _():
-        cext[cx + 2 : cx + 4] = jnp.zeros((2, yw, cz), f32)
+    for dj, dd in sides:
+
+        @pl.when(beside[-dj, -dd])
+        def _(dj=dj, dd=dd):
+            halo_copies[dj, dd].wait_recv()
 
     count_x = fx + 2 * HALO
     zi, zo = iota((cz, fz), 0), iota((cz, fz), 1)
@@ -348,7 +356,7 @@
     refine_z = weights((cz, fz), ((zi == zm, 0.75), (zi == zn, 0.25))).astype(bf16)
     refine_z = jnp.concatenate([refine_z, refine_z], axis=0)
     yo = iota((fw, yw), 0) + ystart
-    yi = iota((fw, yw), 1) + wstart
+    yi = iota((fw, yw), 1) + (yc * q - 8)
     ym = yo >> 1
     yn = ym + ((yo & 1) << 1) - 1
     grid = jnp.logical_and(yo >= 0, yo < fy)
@@ -448,26 +456,30 @@
         result = jnp.dot(
             jnp.concatenate([high, low], axis=1).astype(bf16), restrict_z, preferred_element_type=f32
         )
-        out[low_row:high_row, pl.ds(ymine, yc), :] = result.reshape(high_row - low_row, yc, cz)
-
-    base = j - q
+        mine[low_row:high_row] = result.reshape(high_row - low_row, yc, cz)
+
     half = cx // 2
     gather = []
+    keep = []
     done = 0
     for piece, (low_row, high_row) in enumerate(((0, half), (half, cx))):
-        lax.fori_loop(done, 2 * high_row + 4, exchange_row, 0)
+        lax.fori_loop(done, 2 * high_row + 4, exchange_row, 0, unroll=2)
         done = 2 * high_row + 4
         restrict_rows(low_row, high_row)
+        rows = pl.ds(low_row, high_row - low_row)
+        at = (rows, pl.ds(ymine, yc), slice(None))
         for k in range(1, Q):
-            at = (pl.ds(low_row, high_row - low_row), pl.ds(ymine, yc), slice(None))
             copy = pltpu.make_async_remote_copy(
-                src_ref=out.at[at],
+                src_ref=mine.at[rows],
                 dst_ref=out.at[at],
                 send_sem=gs_sem.at[piece, k - 1], recv_sem=gr_sem.at[piece, k - 1],
                 device_id=(base + lax.rem(q + k, Q), d), device_id_type=MESH,
             )
             copy.start()
             gather.append(copy)
+        copy = pltpu.make_async_copy(mine.at[rows], out.at[at], keep_sem.at[piece])
+        copy.start()
+        keep.append(copy)
     for copy in part_copies:
         copy.wait_send()
     for k in (1, 2, 3):
@@ -477,15 +489,13 @@
             offset_copies[k].wait_send()
             block_copies[k].wait_send()
 
-    @pl.when(inside[1])
-    def _():
-        rise.wait_send()
-
-    @pl.when(inside[-1])
-    def _():
-        sink.wait_send()
-
-    for copy in gather:
+    for dj, dd in sides:
+
+        @pl.when(beside[dj, dd])
+        def _(dj=dj, dd=dd):
+            halo_copies[dj, dd].wait_send()
+
+    for copy in gather + keep:
         copy.wait()
 
 
@@ -503,17 +513,17 @@
         functools.partial(kernel, G, N, Q),
         out_shape=jax.ShapeDtypeStruct((cx, cy, cz), f32),
         in_specs=[hbm, vmem, hbm, smem, smem],
-        out_specs=vmem,
+        out_specs=hbm,
         scratch_shapes=[
             pltpu.VMEM((channels, slots, block), bf16),
-            pltpu.VMEM((cx, yw, cz), f32),
-            pltpu.VMEM((G - 1, cx, yw, cz), f32),
+            pltpu.VMEM((cx, yc, cz), f32),
+            pltpu.VMEM((G - 1, cx, yc, cz), f32),
             pltpu.VMEM((cx + 4, yw, cz), f32),
         ]
         + [pltpu.VMEM((slots, p[1] * GROUP), f32) for p in plan]
         + [pltpu.VMEM((slots, 26 * GROUP), f32)] * 2
         + [pltpu.SMEM((4,) + sphere_offsets.shape, jnp.int32)]
-        + [pltpu.VMEM((2, slots, SPAN, SPAN), bf16), pltpu.VMEM((2, 26 * LINES, slots * 2 * SPAN), bf16)]
+        + [pltpu.VMEM((2, 4, SPAN, 128), bf16), pltpu.VMEM((2, 26 * LINES, slots * 2 * SPAN), bf16)]
         + [pltpu.VMEM((p[2] + 1, 2 * SBY, SPAN), bf16) for p in plan]
         + [
             pltpu.VMEM(((fx + 4) * fw, 2 * SPAN), bf16),
@@ -521,21 +531,23 @@
             pltpu.VMEM((fx + 2 * HALO + 1, fw, fz), f32),
             pltpu.VMEM((fx + 4, fw, fz), f32),
             pltpu.VMEM((fx + 4, fw, fz), f32),
+            pltpu.VMEM((cx, yc, cz), f32),
             pltpu.SemaphoreType.DMA(()),
             pltpu.SemaphoreType.DMA(()),
             pltpu.SemaphoreType.DMA((G - 1,)),
             pltpu.SemaphoreType.DMA((G - 1,)),
-            pltpu.SemaphoreType.DMA((2,)),
-            pltpu.SemaphoreType.DMA((2,)),
+            pltpu.SemaphoreType.DMA((8,)),
+            pltpu.SemaphoreType.DMA((8,)),
             pltpu.SemaphoreType.DMA((4,)),
             pltpu.SemaphoreType.DMA((4,)),
             pltpu.SemaphoreType.DMA((4,)),
             pltpu.SemaphoreType.DMA((4,)),
             pltpu.SemaphoreType.DMA((2, Q - 1)),
             pltpu.SemaphoreType.DMA((2, Q - 1)),
+            pltpu.SemaphoreType.DMA((2,)),
         ],
         compiler_params=pltpu.CompilerParams(
-            collective_id=0, has_side_effects=True, vmem_limit_bytes=40 * 1024 * 1024
+            collective_id=0, has_side_effects=True, vmem_limit_bytes=58 * 1024 * 1024
         ),
     )(partial_density, moments.T, shape_functions.transpose(1, 0, 2), sphere_offsets, owned_count)
 

time: 30 us -> 25.2 us (0.84)
  Pallas kernels: 25.5 us -> 22.7 us
  local copies, waits for them, and re-layouts: 3.55 us -> 1.69 us
    pallas_call x1, Pallas kernels: 25.5 us -> 22.7 us  [body(): pl.pallas_call(functools.partial(kernel, G, N, Q), out_shape=jax.ShapeDty...]
    unnamed x9 -> x1, local copies, waits for them, and re-layouts: 3.55 us -> 1.69 us
where the time goes in v4:
time: 25.2 us; the launch traced here: 25.1 us
  Pallas kernels  22.7 us (90%)
  local copies, waits for them, and re-layouts  1.69 us (7%)
  between operations  0.66 us (3%)
    pallas_call x1, Pallas kernels, body(): pl.pallas_call(functools.partial(kernel, G, N, Q), out_shape=jax.ShapeDty...  22.7 us
    unnamed x1, local copies, waits for them, and re-layouts  1.69 us

profile of v4, /device:TPU:0, one launch (start us, length us, event | category | flops | bytes accessed | tf_op | source)
XLA Modules:
  0.0 25.1 jit_solution(13968599808309785631)
XLA Ops:
  0.7 22.7 %shard_map.55 = f32[6,96,128]{2,1,0:T(8,128)} custom-call(f32[1,6,96,128]{3,2,1,0:T(8,128)} %part.1, bf16[8,9]{1,0:T(8,128)(2,1)} %bitcast.3, bf16[9,8,6912]{2,1,0:T(8,128)(2,1)} %bitcast.2, s32[3,8]{1,0:T(4,128)} %off.1, s32[1]{0:T(128)S(6)} %copy.7.cnt), custom_call_target="tpu_custom_call" | custom-call | tf_op jit(solution)/shard_map/pallas_call | solution.py:512
  23.4 1.7 %copy.8 = f32[6,96,128]{2,1,0:T(8,128)} copy(f32[6,96,128]{2,1,0:T(8,128)} %shard_map.55) | data formatting | bytes 589824

commit v5 on v4

--- a/solution.py
+++ b/solution.py
@@ -14,6 +14,7 @@
 LINES = 8
 SPAN = 256
 SLOT_LANES = 32
+PIECES = 3
 HALO = 3
 
 kappa_pbe = 0.804
@@ -54,10 +55,10 @@
 
 def kernel(
     G, N, Q,
-    part, mom, shp_hbm, off, cnt,
+    part, mom_hbm, shp_hbm, off_hbm, cnt_hbm,
     out,
-    shp, win, recv, cext, v0, v1, v2, v3, vh, vl, offs, unfolder, wide, u0, u1, u2, u3, lined, lined_coarse, dens, flux, pot, mine,
-    shp_sem, win_sem, ps_sem, pr_sem, cs_sem, cr_sem, vs_sem, vr_sem, os_sem, or_sem, gs_sem, gr_sem, keep_sem,
+    mom, off, cnt, shp, win, recv, cext, v0, v1, v2, v3, vh, vl, offs, unfolder, wide, u0, u1, u2, u3, lined, lined_coarse, dens, flux, pot, mine,
+    small_sem, shp_sem, win_sem, ps_sem, pr_sem, cs_sem, cr_sem, vs_sem, vr_sem, os_sem, or_sem, gs_sem, gr_sem, keep_sem,
 ):
     _, cx, cy, cz = part.shape
     fx, fy, fz = 2 * cx, 2 * cy, 2 * cz
@@ -73,8 +74,16 @@
 
     own = pltpu.make_async_copy(part.at[0, :, chunk_of(j), :], win, win_sem)
     own.start()
-    fetch = pltpu.make_async_copy(shp_hbm, shp, shp_sem)
-    fetch.start()
+    small = []
+    for n, (source, target) in enumerate(((mom_hbm, mom), (off_hbm, off), (cnt_hbm, cnt))):
+        small.append(pltpu.make_async_copy(source, target, small_sem.at[n]))
+        small[-1].start()
+    piece_lanes = shp.shape[2] // PIECES
+    fetches = []
+    for n in range(PIECES):
+        at = (slice(None), slice(None), pl.ds(n * piece_lanes, piece_lanes))
+        fetches.append(pltpu.make_async_copy(shp_hbm.at[at], shp.at[at], shp_sem.at[n]))
+        fetches[-1].start()
     cext[...] = jnp.zeros(cext.shape, f32)
     base = j - q
     ystart = 2 * yc * q - 4
@@ -126,31 +135,14 @@
         part_copies.append(copy)
 
     channels = shp.shape[0]
-    moments = mom[...].astype(f32)
-    moments = jnp.where(iota(moments.shape, 0) < cnt[0], moments, 0.0)
-    scales = [jnp.broadcast_to(moments[:, l : l + 1], (slots, GROUP)) for l in range(channels)]
-    fetch.wait()
-    for g in range(v0.shape[1] // GROUP):
-        at = slice(g * GROUP, (g + 1) * GROUP)
-        total = shp[0, :, at].astype(f32) * scales[0]
-        for l in range(1, channels):
-            total = total + shp[l, :, at].astype(f32) * scales[l]
-        v0[:, at] = total
-
+    for copy in small:
+        copy.wait()
     plan = sources(fx)
     blocks = (v0, v1, v2, v3)
     folded = (u0, u1, u2, u3)
-    block_copies = [None]
     offset_copies = [None]
     for k in (1, 2, 3):
-        lane, groups = plan[k][0], plan[k][1]
         step = -plan[k][6]
-        block_copies.append(pltpu.make_async_remote_copy(
-            src_ref=v0.at[:, pl.ds(lane, groups * GROUP)],
-            dst_ref=blocks[k],
-            send_sem=vs_sem.at[k], recv_sem=vr_sem.at[k],
-            device_id=(j, d + step), device_id_type=MESH,
-        ))
         offset_copies.append(pltpu.make_async_remote_copy(
             src_ref=off,
             dst_ref=offs.at[k],
@@ -161,7 +153,38 @@
         @pl.when(inside[step])
         def _(k=k):
             offset_copies[k].start()
-            block_copies[k].start()
+
+    last = shp.shape[2] - plan[2][1] * GROUP
+    cuts = [[(1, n * piece_lanes, n * piece_lanes, piece_lanes)] for n in range(PIECES)]
+    cuts[0].append((3, 0, 0, plan[3][1] * GROUP))
+    cuts[PIECES - 1].append((2, last, 0, plan[2][1] * GROUP))
+    block_copies = {1: [], 2: [], 3: []}
+    moments = mom[...].astype(f32)
+    moments = jnp.where(iota(moments.shape, 0) < cnt[0], moments, 0.0)
+    scales = [jnp.broadcast_to(moments[:, l : l + 1], (slots, GROUP)) for l in range(channels)]
+    sent = 0
+    for n in range(PIECES):
+        fetches[n].wait()
+        for g in range(n * piece_lanes // GROUP, (n + 1) * piece_lanes // GROUP):
+            at = slice(g * GROUP, (g + 1) * GROUP)
+            total = shp[0, :, at].astype(f32) * scales[0]
+            for l in range(1, channels):
+                total = total + shp[l, :, at].astype(f32) * scales[l]
+            v0[:, at] = total
+        for k, lane, there, lanes in cuts[n]:
+            step = -plan[k][6]
+            copy = pltpu.make_async_remote_copy(
+                src_ref=v0.at[:, pl.ds(lane, lanes)],
+                dst_ref=blocks[k].at[:, pl.ds(there, lanes)],
+                send_sem=vs_sem.at[sent], recv_sem=vr_sem.at[sent],
+                device_id=(j, d + step), device_id_type=MESH,
+            )
+            block_copies[k].append(copy)
+            sent += 1
+
+            @pl.when(inside[step])
+            def _(copy=copy):
+                copy.start()
 
     line_masks = []
     for h in range(2):
@@ -300,22 +323,6 @@
     unfold((0,))
     place(0, True)
 
-    for k in (1, 2, 3):
-
-        @pl.when(inside[plan[k][6]])
-        def _(k=k):
-            offset_copies[k].wait_recv()
-            block_copies[k].wait_recv()
-
-        @pl.when(jnp.logical_not(inside[plan[k][6]]))
-        def _(k=k):
-            blocks[k][...] = jnp.zeros(blocks[k].shape, f32)
-            for row in range(3):
-                for s in range(slots):
-                    offs[k, row, s] = 0
-
-    unfold((1, 2, 3))
-
     own.wait()
     for copy in part_copies:
         copy.wait_recv()
@@ -339,6 +346,23 @@
         @pl.when(beside[dj, dd])
         def _(dj=dj, dd=dd):
             halo_copies[dj, dd].start()
+
+    for k in (1, 2, 3):
+
+        @pl.when(inside[plan[k][6]])
+        def _(k=k):
+            offset_copies[k].wait_recv()
+            for copy in block_copies[k]:
+                copy.wait_recv()
+
+        @pl.when(jnp.logical_not(inside[plan[k][6]]))
+        def _(k=k):
+            blocks[k][...] = jnp.zeros(blocks[k].shape, f32)
+            for row in range(3):
+                for s in range(slots):
+                    offs[k, row, s] = 0
+
+    unfold((1, 2, 3))
 
     for k in (1, 2, 3):
         place(k, False)
@@ -458,11 +482,12 @@
         )
         mine[low_row:high_row] = result.reshape(high_row - low_row, yc, cz)
 
-    half = cx // 2
     gather = []
     keep = []
     done = 0
-    for piece, (low_row, high_row) in enumerate(((0, half), (half, cx))):
+    for piece, (low_row, high_row) in enumerate(
+        (cx * n // PIECES, cx * (n + 1) // PIECES) for n in range(PIECES)
+    ):
         lax.fori_loop(done, 2 * high_row + 4, exchange_row, 0, unroll=2)
         done = 2 * high_row + 4
         restrict_rows(low_row, high_row)
@@ -487,7 +512,8 @@
         @pl.when(inside[-plan[k][6]])
         def _(k=k):
             offset_copies[k].wait_send()
-            block_copies[k].wait_send()
+            for copy in block_copies[k]:
+                copy.wait_send()
 
     for dj, dd in sides:
 
@@ -506,15 +532,16 @@
     yc = cy // Q
     yw, fw = yc + 16, 2 * yc + 8
     plan = sources(fx)
-    hbm = pl.BlockSpec(memory_space=pltpu.HBM)
-    vmem = pl.BlockSpec(memory_space=pltpu.VMEM)
-    smem = pl.BlockSpec(memory_space=pltpu.SMEM)
+    hbm = pl.BlockSpec(memory_space=pl.ANY)
     return pl.pallas_call(
         functools.partial(kernel, G, N, Q),
         out_shape=jax.ShapeDtypeStruct((cx, cy, cz), f32),
-        in_specs=[hbm, vmem, hbm, smem, smem],
+        in_specs=[hbm] * 5,
         out_specs=hbm,
         scratch_shapes=[
+            pltpu.VMEM((slots, channels), bf16),
+            pltpu.SMEM(sphere_offsets.shape, jnp.int32),
+            pltpu.SMEM((1,), jnp.int32),
             pltpu.VMEM((channels, slots, block), bf16),
             pltpu.VMEM((cx, yc, cz), f32),
             pltpu.VMEM((G - 1, cx, yc, cz), f32),
@@ -532,19 +559,20 @@
             pltpu.VMEM((fx + 4, fw, fz), f32),
             pltpu.VMEM((fx + 4, fw, fz), f32),
             pltpu.VMEM((cx, yc, cz), f32),
-            pltpu.SemaphoreType.DMA(()),
+            pltpu.SemaphoreType.DMA((3,)),
+            pltpu.SemaphoreType.DMA((PIECES,)),
             pltpu.SemaphoreType.DMA(()),
             pltpu.SemaphoreType.DMA((G - 1,)),
             pltpu.SemaphoreType.DMA((G - 1,)),
             pltpu.SemaphoreType.DMA((8,)),
             pltpu.SemaphoreType.DMA((8,)),
+            pltpu.SemaphoreType.DMA((PIECES + 2,)),
+            pltpu.SemaphoreType.DMA((PIECES + 2,)),
             pltpu.SemaphoreType.DMA((4,)),
             pltpu.SemaphoreType.DMA((4,)),
-            pltpu.SemaphoreType.DMA((4,)),
-            pltpu.SemaphoreType.DMA((4,)),
-            pltpu.SemaphoreType.DMA((2, Q - 1)),
-            pltpu.SemaphoreType.DMA((2, Q - 1)),
-            pltpu.SemaphoreType.DMA((2,)),
+            pltpu.SemaphoreType.DMA((PIECES, Q - 1)),
+            pltpu.SemaphoreType.DMA((PIECES, Q - 1)),
+            pltpu.SemaphoreType.DMA((PIECES,)),
         ],
         compiler_params=pltpu.CompilerParams(
             collective_id=0, has_side_effects=True, vmem_limit_bytes=58 * 1024 * 1024

time: 25.2 us -> 24.8 us (0.984)
  Pallas kernels: 22.7 us -> 22.3 us
    pallas_call x1, Pallas kernels: 22.7 us -> 22.3 us  [body(): pl.pallas_call(functools.partial(kernel, G, N, Q), out_shape=jax.ShapeDty...]
where the time goes in v5:
time: 24.8 us; the launch traced here: 24.6 us
  Pallas kernels  22.3 us (90%)
  local copies, waits for them, and re-layouts  1.69 us (7%)
  between operations  0.66 us (3%)
    pallas_call x1, Pallas kernels, body(): pl.pallas_call(functools.partial(kernel, G, N, Q), out_shape=jax.ShapeDty...  22.3 us
    unnamed x1, local copies, waits for them, and re-layouts  1.69 us

profile of v5, /device:TPU:0, one launch (start us, length us, event | category | flops | bytes accessed | tf_op | source)
XLA Modules:
  0.0 24.6 jit_solution(2469785622673309528)
XLA Ops:
  0.7 22.3 %shard_map.55 = f32[6,96,128]{2,1,0:T(8,128)} custom-call(f32[1,6,96,128]{3,2,1,0:T(8,128)} %part.1, bf16[8,9]{1,0:T(8,128)(2,1)} %bitcast.3, bf16[9,8,6912]{2,1,0:T(8,128)(2,1)} %bitcast.2, s32[3,8]{1,0:T(4,128)} %off_hbm.1, s32[1]{0:T(128)S(6)} %copy.7.cnt_hbm), custom_call_target="tpu_custom_call" | custom-call | tf_op jit(solution)/shard_map/pallas_call | solution.py:536
  23.0 1.7 %copy.8 = f32[6,96,128]{2,1,0:T(8,128)} copy(f32[6,96,128]{2,1,0:T(8,128)} %shard_map.55) | data formatting | bytes 589824

commit v6 on v5

--- a/solution.py
+++ b/solution.py
@@ -22,6 +22,7 @@
 exchange_prefactor = -0.75 * (3.0 / 3.141592653589793) ** (1.0 / 3.0)
 gradient_scale = 4.0 * (3.0 * 3.141592653589793**2) ** (2.0 / 3.0)
 half_inverse = 0.5 / 0.2
+log2_e = 1.4426950408889634
 
 f32 = jnp.float32
 bf16 = jnp.bfloat16
@@ -414,13 +415,22 @@
         for i in range(3):
             dens[start + i] = (dens[start + i] + value[i]) * in_grid(start + i - HALO)
 
-    lanes = iota((fw, fz), 1)
-    first_lane, last_lane = lanes == 0, lanes == fz - 1
+    lanes = iota((fw, 128), 1)
+    first_lane, last_lane = lanes == 0, lanes == 127
+    tiles = fz // 128
 
     def diff_z(f):
-        after = jnp.where(last_lane, 0.0, pltpu.roll(f, fz - 1, 1))
-        before = jnp.where(first_lane, 0.0, pltpu.roll(f, 1, 1))
-        return after - before
+        parts = [f[:, 128 * t : 128 * t + 128] for t in range(tiles)]
+        ahead = [pltpu.roll(part, 127, 1) for part in parts] + [0.0]
+        behind = [0.0] + [pltpu.roll(part, 1, 1) for part in parts]
+        return jnp.concatenate(
+            [
+                jnp.where(last_lane, ahead[t + 1], ahead[t])
+                - jnp.where(first_lane, behind[t], behind[t + 1])
+                for t in range(tiles)
+            ],
+            axis=1,
+        )
 
     def diff_y(f):
         return pltpu.roll(f, fw - 1, 0) - pltpu.roll(f, 1, 0)
@@ -433,15 +443,18 @@
         sigma = gx * gx + gy * gy + gz * gz
         live = n > 0.0
         log_n = jnp.log(jnp.where(live, n, 1.0))
-        cube_root = jnp.exp(log_n * (1.0 / 3.0))
-        inv_ft = jnp.exp(log_n * (-4.0 / 3.0))
-        reduced = sigma * (inv_ft * inv_ft) * (half_inverse * half_inverse / gradient_scale)
-        inv_d = 1.0 / (1.0 + (mu_pbe / kappa_pbe) * reduced)
-        slope = mu_pbe * inv_d * inv_d
-        by_density = (exchange_prefactor * cube_root) * (
-            (4.0 / 3.0) * (1.0 + kappa_pbe - kappa_pbe * inv_d) - (8.0 / 3.0) * reduced * slope
+        cube_root = jnp.exp2(log_n * (log2_e / 3.0))
+        inv_ft = jnp.exp2(log_n * (-4.0 * log2_e / 3.0))
+        scale = half_inverse * half_inverse * mu_pbe / (kappa_pbe * gradient_scale)
+        inv_d = 1.0 / (1.0 + sigma * (inv_ft * inv_ft * scale))
+        inv_d2 = inv_d * inv_d
+        by_density = cube_root * (
+            exchange_prefactor * 4.0 / 3.0 * (1.0 + kappa_pbe)
+            - (exchange_prefactor * 4.0 * kappa_pbe) * inv_d
+            + (exchange_prefactor * 8.0 / 3.0 * kappa_pbe) * inv_d2
         )
-        twice = jnp.where(live, (2.0 * exchange_prefactor * half_inverse * half_inverse / gradient_scale) * slope * inv_ft, 0.0)
+        twice = 2.0 * exchange_prefactor * half_inverse * half_inverse * mu_pbe / gradient_scale
+        twice = jnp.where(live, (twice * inv_ft) * inv_d2, 0.0)
         flux[i] = twice * gx
         pot[i] = by_density - (diff_y(twice * gy) + diff_z(twice * gz))
         return carry
@@ -575,7 +588,7 @@
             pltpu.SemaphoreType.DMA((PIECES,)),
         ],
         compiler_params=pltpu.CompilerParams(
-            collective_id=0, has_side_effects=True, vmem_limit_bytes=58 * 1024 * 1024
+            collective_id=0, has_side_effects=True, vmem_limit_bytes=54900 * 1024
         ),
     )(partial_density, moments.T, shape_functions.transpose(1, 0, 2), sphere_offsets, owned_count)
 

time: 24.8 us -> 24.4 us (0.984)
  local copies, waits for them, and re-layouts: 1.69 us -> 1.39 us
    unnamed x1 -> x5, local copies, waits for them, and re-layouts: 1.69 us -> 1.39 us
where the time goes in v6:
time: 24.4 us; the launch traced here: 24.2 us
  Pallas kernels  22.1 us (91%)
  local copies, waits for them, and re-layouts  1.39 us (6%)
  between operations  0.69 us (3%)
    pallas_call x1, Pallas kernels, body(): pl.pallas_call(functools.partial(kernel, G, N, Q), out_shape=jax.ShapeDty...  22.1 us
    unnamed x5, local copies, waits for them, and re-layouts  1.39 us

profile of v6, /device:TPU:0, one launch (start us, length us, event | category | flops | bytes accessed | tf_op | source)
XLA Modules:
  0.0 24.2 jit_solution(10676234922357131556)
XLA Ops:
  0.0 0.0 copy-start.1
  0.7 0.0 copy-start
  0.7 0.0 copy-done.1
  0.7 0.7 %copy-done = bf16[9,8]{0,1:T(8,128)(2,1)S(1)} copy-done((bf16[9,8]{0,1:T(8,128)(2,1)S(1)}, bf16[9,8]{0,1:T(8,128)(2,1)}, u32[]{:S(2)}) %copy-start) | copy-done | bytes 168
  1.4 22.1 %shard_map.55 = f32[6,96,128]{2,1,0:T(8,128)S(1)} custom-call(f32[1,6,96,128]{3,2,1,0:T(8,128)} %part.1, bf16[8,9]{1,0:T(8,128)(2,1)S(1)} %bitcast.2, bf16[9,8,6912]{2,1,0:T(8,128)(2,1)} %bitcast.3, s32[3,8]{1,0:T(4,128)S(1)} %copy-done.1, s32[1]{0:T(128)S(6)} %copy.7.cnt_hbm), custom_call_target="tpu_custom_call" | custom-call | tf_op jit(solution)/shard_map/pallas_call | solution.py:549
  23.5 0.7 %copy.8 = f32[6,96,128]{2,1,0:T(8,128)} copy(f32[6,96,128]{2,1,0:T(8,128)S(1)} %shard_map.55) | data formatting | bytes 589824
Async XLA Ops:
  0.0 0.7 %copy-start.1 = (s32[3,8]{1,0:T(4,128)S(1)}, s32[3,8]{1,0:T(4,128)}, u32[]{:S(2)}) copy-start(s32[3,8]{1,0:T(4,128)} %off_hbm.1) | copy-start | bytes 292
  0.7 0.7 %copy-start = (bf16[9,8]{0,1:T(8,128)(2,1)S(1)}, bf16[9,8]{0,1:T(8,128)(2,1)}, u32[]{:S(2)}) copy-start(bf16[9,8]{0,1:T(8,128)(2,1)} %param.6) | copy-start | bytes 436

commit v7 on v6

--- a/solution.py
+++ b/solution.py
@@ -58,7 +58,7 @@
     G, N, Q,
     part, mom_hbm, shp_hbm, off_hbm, cnt_hbm,
     out,
-    mom, off, cnt, shp, win, recv, cext, v0, v1, v2, v3, vh, vl, offs, unfolder, wide, u0, u1, u2, u3, lined, lined_coarse, dens, flux, pot, mine,
+    mom, off, cnt, shp, win, recv, cext, v0, v1, v2, v3, vh, vl, offs, unfolder, wide, u0, u1, u2, u3, lined, lined_coarse, dens, flux, flux_y, pot, mine,
     small_sem, shp_sem, win_sem, ps_sem, pr_sem, cs_sem, cr_sem, vs_sem, vr_sem, os_sem, or_sem, gs_sem, gr_sem, keep_sem,
 ):
     _, cx, cy, cz = part.shape
@@ -86,6 +86,10 @@
         fetches.append(pltpu.make_async_copy(shp_hbm.at[at], shp.at[at], shp_sem.at[n]))
         fetches[-1].start()
     cext[...] = jnp.zeros(cext.shape, f32)
+    for lines in (dens, flux_y):
+        edge = jnp.zeros((lines.shape[0], 8, fz), f32)
+        lines[:, 0:8] = edge
+        lines[:, fw + 8 : fw + 16] = edge
     base = j - q
     ystart = 2 * yc * q - 4
     slots = shp.shape[1]
@@ -316,11 +320,12 @@
             ).reshape(size, fw, fz)
             at = x0 + HALO + start
             if first:
-                dens[at : at + size] = value
+                dens[at : at + size, window] = value
             else:
-                dens[at : at + size] = dens[at : at + size] + value
-
-    dens[0:HALO] = jnp.zeros((HALO, fw, fz), f32)
+                dens[at : at + size, window] = dens[at : at + size, window] + value
+
+    window = slice(8, fw + 8)
+    dens[0:HALO, window] = jnp.zeros((HALO, fw, fz), f32)
     unfold((0,))
     place(0, True)
 
@@ -413,9 +418,9 @@
             lined_coarse[start * fw : (start + 3) * fw, :], refine_z, preferred_element_type=f32
         ).reshape(3, fw, fz)
         for i in range(3):
-            dens[start + i] = (dens[start + i] + value[i]) * in_grid(start + i - HALO)
-
-    lanes = iota((fw, 128), 1)
+            dens[start + i, window] = (dens[start + i, window] + value[i]) * in_grid(start + i - HALO)
+
+    lanes = iota((8, 128), 1)
     first_lane, last_lane = lanes == 0, lanes == 127
     tiles = fz // 128
 
@@ -432,13 +437,17 @@
             axis=1,
         )
 
-    def diff_y(f):
-        return pltpu.roll(f, fw - 1, 0) - pltpu.roll(f, 1, 0)
-
     def exchange_row(i, carry):
-        n = dens[i + 1]
-        gx = dens[i + 2] - dens[i]
-        gy = diff_y(n)
+        for line in range(0, fw, 8):
+            exchange_tile(i, line)
+        return carry
+
+    def exchange_tile(i, line):
+        at = slice(line, line + 8)
+        here = slice(line + 8, line + 16)
+        n = dens[i + 1, here]
+        gx = dens[i + 2, here] - dens[i, here]
+        gy = dens[i + 1, line + 9 : line + 17] - dens[i + 1, line + 7 : line + 15]
         gz = diff_z(n)
         sigma = gx * gx + gy * gy + gz * gz
         live = n > 0.0
@@ -455,9 +464,9 @@
         )
         twice = 2.0 * exchange_prefactor * half_inverse * half_inverse * mu_pbe / gradient_scale
         twice = jnp.where(live, (twice * inv_ft) * inv_d2, 0.0)
-        flux[i] = twice * gx
-        pot[i] = by_density - (diff_y(twice * gy) + diff_z(twice * gz))
-        return carry
+        flux[i, at] = twice * gx
+        flux_y[i, here] = twice * gy
+        pot[i, at] = by_density - diff_z(twice * gz)
 
 
     ro, ri = iota((yc, fw), 0), iota((yc, fw), 1)
@@ -473,8 +482,11 @@
     restrict_z = weights((fz, cz), ((inner, 0.375), (outer, 0.125))).astype(bf16)
     restrict_z = jnp.concatenate([restrict_z, restrict_z], axis=0)
 
-    def full(x):
-        return (pot[x + 2] - (flux[x + 3] - flux[x + 1])) * in_grid(x)
+    def full(x, line):
+        at = slice(line, line + 8)
+        spread = flux[x + 3, at] - flux[x + 1, at]
+        spread = spread + (flux_y[x + 2, line + 9 : line + 17] - flux_y[x + 2, line + 7 : line + 15])
+        return (pot[x + 2, at] - spread) * in_grid(x)
 
     ymine = pl.multiple_of(q * yc, 8)
 
@@ -482,11 +494,16 @@
         pieces = []
         for i in range(low_row, high_row):
             x = 2 * i
-            mixed = 0.125 * (full(x - 1) + full(x + 2)) + 0.375 * (full(x) + full(x + 1))
-            high, low = split(mixed)
+            high, low = [], []
+            for line in range(0, fw, 8):
+                mixed = 0.125 * (full(x - 1, line) + full(x + 2, line))
+                mixed = mixed + 0.375 * (full(x, line) + full(x + 1, line))
+                upper, lower = split(mixed)
+                high.append(upper)
+                low.append(lower)
             pieces.append(jnp.dot(
                 restrict_y,
-                jnp.concatenate([high, low], axis=0).astype(bf16),
+                jnp.concatenate(high + low, axis=0).astype(bf16),
                 preferred_element_type=f32,
             ))
         high, low = split(jnp.concatenate(pieces, axis=0))
@@ -568,8 +585,9 @@
         + [
             pltpu.VMEM(((fx + 4) * fw, 2 * SPAN), bf16),
             pltpu.VMEM(((fx + 2 * HALO) * fw, 2 * cz), bf16),
-            pltpu.VMEM((fx + 2 * HALO + 1, fw, fz), f32),
+            pltpu.VMEM((fx + 2 * HALO + 1, fw + 16, fz), f32),
             pltpu.VMEM((fx + 4, fw, fz), f32),
+            pltpu.VMEM((fx + 4, fw + 16, fz), f32),
             pltpu.VMEM((fx + 4, fw, fz), f32),
             pltpu.VMEM((cx, yc, cz), f32),
             pltpu.SemaphoreType.DMA((3,)),

time: 24.4 us -> 24.5 us (level)
  no operation moved by 1% of the time
where the time goes in v7:
time: 24.5 us; the launch traced here: 24.3 us
  Pallas kernels  22.3 us (91%)
  local copies, waits for them, and re-layouts  1.39 us (6%)
  between operations  0.69 us (3%)
    pallas_call x1, Pallas kernels, body(): pl.pallas_call(functools.partial(kernel, G, N, Q), out_shape=jax.ShapeDty...  22.3 us
    unnamed x5, local copies, waits for them, and re-layouts  1.39 us

profile of v7, /device:TPU:0, one launch (start us, length us, event | category | flops | bytes accessed | tf_op | source)
XLA Modules:
  0.0 24.3 jit_solution(15238236230490156063)
XLA Ops:
  0.0 0.0 copy-start.1
  0.7 0.0 copy-start
  0.7 0.0 copy-done.1
  0.7 0.7 %copy-done = bf16[9,8]{0,1:T(8,128)(2,1)S(1)} copy-done((bf16[9,8]{0,1:T(8,128)(2,1)S(1)}, bf16[9,8]{0,1:T(8,128)(2,1)}, u32[]{:S(2)}) %copy-start) | copy-done | bytes 168
  1.4 22.3 %shard_map.55 = f32[6,96,128]{2,1,0:T(8,128)S(1)} custom-call(f32[1,6,96,128]{3,2,1,0:T(8,128)} %part.1, bf16[8,9]{1,0:T(8,128)(2,1)S(1)} %bitcast.2, bf16[9,8,6912]{2,1,0:T(8,128)(2,1)} %bitcast.3, s32[3,8]{1,0:T(4,128)S(1)} %copy-done.1, s32[1]{0:T(128)S(6)} %copy.7.cnt_hbm), custom_call_target="tpu_custom_call" | custom-call | tf_op jit(solution)/shard_map/pallas_call | solution.py:566
  23.6 0.7 %copy.8 = f32[6,96,128]{2,1,0:T(8,128)} copy(f32[6,96,128]{2,1,0:T(8,128)S(1)} %shard_map.55) | data formatting | bytes 589824
Async XLA Ops:
  0.0 0.7 %copy-start.1 = (s32[3,8]{1,0:T(4,128)S(1)}, s32[3,8]{1,0:T(4,128)}, u32[]{:S(2)}) copy-start(s32[3,8]{1,0:T(4,128)} %off_hbm.1) | copy-start | bytes 292
  0.7 0.7 %copy-start = (bf16[9,8]{0,1:T(8,128)(2,1)S(1)}, bf16[9,8]{0,1:T(8,128)(2,1)}, u32[]{:S(2)}) copy-start(bf16[9,8]{0,1:T(8,128)(2,1)} %param.6) | copy-start | bytes 436

commit v8 on v6

--- a/solution.py
+++ b/solution.py
@@ -47,10 +47,10 @@
 
 def sources(fx):
     return (
-        (0, 18, SBX, 0, 0, fx + HALO, 0),
-        (0, 18, SBX, 0, -HALO, SBX - 1 + HALO, -1),
-        (5760, 3, 2, 10, -HALO, 2, -2),
-        (0, 5, 3, 0, fx, HALO, 1),
+        (SBX, 0, 0, fx + HALO, 0),
+        (SBX, 0, -HALO, SBX - 1 + HALO, -1),
+        (2, SBX - 2, -HALO, 2, -2),
+        (HALO, 0, fx, HALO, 1),
     )
 
 
@@ -58,7 +58,7 @@
     G, N, Q,
     part, mom_hbm, shp_hbm, off_hbm, cnt_hbm,
     out,
-    mom, off, cnt, shp, win, recv, cext, v0, v1, v2, v3, vh, vl, offs, unfolder, wide, u0, u1, u2, u3, lined, lined_coarse, dens, flux, pot, mine,
+    mom, off, cnt, shp, win, recv, cext, vh, vl, offs, unfolder, wide, u0, u1, u2, u3, b0, b1, b2, b3, lined, lined_coarse, dens, flux, pot, mine,
     small_sem, shp_sem, win_sem, ps_sem, pr_sem, cs_sem, cr_sem, vs_sem, vr_sem, os_sem, or_sem, gs_sem, gr_sem, keep_sem,
 ):
     _, cx, cy, cz = part.shape
@@ -139,11 +139,11 @@
     for copy in small:
         copy.wait()
     plan = sources(fx)
-    blocks = (v0, v1, v2, v3)
+    blocks = (b0, b1, b2, b3)
     folded = (u0, u1, u2, u3)
     offset_copies = [None]
     for k in (1, 2, 3):
-        step = -plan[k][6]
+        step = -plan[k][4]
         offset_copies.append(pltpu.make_async_remote_copy(
             src_ref=off,
             dst_ref=offs.at[k],
@@ -155,15 +155,9 @@
         def _(k=k):
             offset_copies[k].start()
 
-    last = shp.shape[2] - plan[2][1] * GROUP
-    cuts = [[(1, n * piece_lanes, n * piece_lanes, piece_lanes)] for n in range(PIECES)]
-    cuts[0].append((3, 0, 0, plan[3][1] * GROUP))
-    cuts[PIECES - 1].append((2, last, 0, plan[2][1] * GROUP))
-    block_copies = {1: [], 2: [], 3: []}
     moments = mom[...].astype(f32)
     moments = jnp.where(iota(moments.shape, 0) < cnt[0], moments, 0.0)
     scales = [jnp.broadcast_to(moments[:, l : l + 1], (slots, GROUP)) for l in range(channels)]
-    sent = 0
     for n in range(PIECES):
         fetches[n].wait()
         for g in range(n * piece_lanes // GROUP, (n + 1) * piece_lanes // GROUP):
@@ -171,21 +165,7 @@
             total = shp[0, :, at].astype(f32) * scales[0]
             for l in range(1, channels):
                 total = total + shp[l, :, at].astype(f32) * scales[l]
-            v0[:, at] = total
-        for k, lane, there, lanes in cuts[n]:
-            step = -plan[k][6]
-            copy = pltpu.make_async_remote_copy(
-                src_ref=v0.at[:, pl.ds(lane, lanes)],
-                dst_ref=blocks[k].at[:, pl.ds(there, lanes)],
-                send_sem=vs_sem.at[sent], recv_sem=vr_sem.at[sent],
-                device_id=(j, d + step), device_id_type=MESH,
-            )
-            block_copies[k].append(copy)
-            sent += 1
-
-            @pl.when(inside[step])
-            def _(copy=copy):
-                copy.start()
+            vh[:, at], vl[:, at] = split(total)
 
     line_masks = []
     for h in range(2):
@@ -201,18 +181,15 @@
     def offset_of(k, row, s):
         return off[row, s] if k == 0 else offs[k, row, s]
 
-    def unfold(which):
-        starts = []
-        total = 0
-        for k in which:
-            starts.append(total)
-            width = plan[k][1] * GROUP
-            high, low = split(blocks[k][...])
-            vh[:, total : total + width] = high
-            vl[:, total : total + width] = low
-            total += width
-        groups = total // GROUP
-
+    def fold(k):
+        na = plan[k][0]
+        high, low = split(blocks[k][...])
+        folded[k][0:na] = jnp.concatenate([high, low], axis=1).astype(bf16)
+        folded[k][na] = jnp.zeros((2 * SBY, SPAN), bf16)
+
+    groups = shp.shape[2] // GROUP
+
+    def unfold():
         def one(s, carry):
             for h in range(2):
                 for t, source in enumerate((vh, vl)):
@@ -246,12 +223,7 @@
             value = jnp.concatenate(value, axis=1)
             halves.append(value.reshape(groups, LINES, SPAN))
         lines = jnp.stack(halves, axis=1).reshape(groups * 2 * LINES, SPAN)
-        for k, start in zip(which, starts):
-            na = plan[k][2]
-            at = start // GROUP * 2 * LINES
-            high, low = split(lines[at : at + na * SBY].reshape(na, SBY, SPAN))
-            folded[k][0:na] = jnp.concatenate([high, low], axis=1).astype(bf16)
-            folded[k][na] = jnp.zeros((2 * SBY, SPAN), bf16)
+        blocks[0][...] = lines.reshape(SBX, SBY, SPAN)
 
     lane_tile = iota((16, 128), 1) >> 5
     slot_masks = []
@@ -260,7 +232,7 @@
         slot_masks.append(jnp.concatenate([mask] * 3, axis=0))
 
     def place(k, first):
-        _, _, na, a0, x0, rows, slab = plan[k]
+        na, a0, x0, rows, slab = plan[k]
         rows += rows % 2
         width = 4 * 2 * SBY
         lane = iota((1, width), 1)
@@ -321,7 +293,22 @@
                 dens[at : at + size] = dens[at : at + size] + value
 
     dens[0:HALO] = jnp.zeros((HALO, fw, fz), f32)
-    unfold((0,))
+    unfold()
+    block_copies = [None]
+    for k in (1, 2, 3):
+        na, a0, _, _, slab = plan[k]
+        block_copies.append(pltpu.make_async_remote_copy(
+            src_ref=b0.at[pl.ds(a0, na)],
+            dst_ref=blocks[k],
+            send_sem=vs_sem.at[k], recv_sem=vr_sem.at[k],
+            device_id=(j, d - slab), device_id_type=MESH,
+        ))
+
+        @pl.when(inside[-slab])
+        def _(k=k):
+            block_copies[k].start()
+
+    fold(0)
     place(0, True)
 
     own.wait()
@@ -348,26 +335,6 @@
         def _(dj=dj, dd=dd):
             halo_copies[dj, dd].start()
 
-    for k in (1, 2, 3):
-
-        @pl.when(inside[plan[k][6]])
-        def _(k=k):
-            offset_copies[k].wait_recv()
-            for copy in block_copies[k]:
-                copy.wait_recv()
-
-        @pl.when(jnp.logical_not(inside[plan[k][6]]))
-        def _(k=k):
-            blocks[k][...] = jnp.zeros(blocks[k].shape, f32)
-            for row in range(3):
-                for s in range(slots):
-                    offs[k, row, s] = 0
-
-    unfold((1, 2, 3))
-
-    for k in (1, 2, 3):
-        place(k, False)
-
     for dj, dd in sides:
 
         @pl.when(beside[-dj, -dd])
@@ -414,6 +381,24 @@
         ).reshape(3, fw, fz)
         for i in range(3):
             dens[start + i] = (dens[start + i] + value[i]) * in_grid(start + i - HALO)
+
+    for k in (3, 1, 2):
+        slab = plan[k][4]
+
+        @pl.when(inside[slab])
+        def _(k=k):
+            offset_copies[k].wait_recv()
+            block_copies[k].wait_recv()
+
+        @pl.when(jnp.logical_not(inside[slab]))
+        def _(k=k):
+            blocks[k][...] = jnp.zeros(blocks[k].shape, f32)
+            for row in range(3):
+                for s in range(slots):
+                    offs[k, row, s] = 0
+
+        fold(k)
+        place(k, False)
 
     lanes = iota((fw, 128), 1)
     first_lane, last_lane = lanes == 0, lanes == 127
@@ -522,11 +507,10 @@
         copy.wait_send()
     for k in (1, 2, 3):
 
-        @pl.when(inside[-plan[k][6]])
+        @pl.when(inside[-plan[k][4]])
         def _(k=k):
             offset_copies[k].wait_send()
-            for copy in block_copies[k]:
-                copy.wait_send()
+            block_copies[k].wait_send()
 
     for dj, dd in sides:
 
@@ -560,11 +544,11 @@
             pltpu.VMEM((G - 1, cx, yc, cz), f32),
             pltpu.VMEM((cx + 4, yw, cz), f32),
         ]
-        + [pltpu.VMEM((slots, p[1] * GROUP), f32) for p in plan]
-        + [pltpu.VMEM((slots, 26 * GROUP), f32)] * 2
+        + [pltpu.VMEM((slots, block), f32)] * 2
         + [pltpu.SMEM((4,) + sphere_offsets.shape, jnp.int32)]
-        + [pltpu.VMEM((2, 4, SPAN, 128), bf16), pltpu.VMEM((2, 26 * LINES, slots * 2 * SPAN), bf16)]
-        + [pltpu.VMEM((p[2] + 1, 2 * SBY, SPAN), bf16) for p in plan]
+        + [pltpu.VMEM((2, 4, SPAN, 128), bf16), pltpu.VMEM((2, block // GROUP * LINES, slots * 2 * SPAN), bf16)]
+        + [pltpu.VMEM((p[0] + 1, 2 * SBY, SPAN), bf16) for p in plan]
+        + [pltpu.VMEM((p[0], SBY, SPAN), f32) for p in plan]
         + [
             pltpu.VMEM(((fx + 4) * fw, 2 * SPAN), bf16),
             pltpu.VMEM(((fx + 2 * HALO) * fw, 2 * cz), bf16),
@@ -579,8 +563,8 @@
             pltpu.SemaphoreType.DMA((G - 1,)),
             pltpu.SemaphoreType.DMA((8,)),
             pltpu.SemaphoreType.DMA((8,)),
-            pltpu.SemaphoreType.DMA((PIECES + 2,)),
-            pltpu.SemaphoreType.DMA((PIECES + 2,)),
+            pltpu.SemaphoreType.DMA((4,)),
+            pltpu.SemaphoreType.DMA((4,)),
             pltpu.SemaphoreType.DMA((4,)),
             pltpu.SemaphoreType.DMA((4,)),
             pltpu.SemaphoreType.DMA((PIECES, Q - 1)),

time: 24.4 us -> 26.6 us (1.090)
  Pallas kernels: 22.1 us -> 24.4 us
    pallas_call x1, Pallas kernels: 22.1 us -> 24.4 us  [body(): pl.pallas_call(functools.partial(kernel, G, N, Q), out_shape=jax.ShapeDty...]
where the time goes in v8:
time: 26.6 us; the launch traced here: 26.4 us
  Pallas kernels  24.4 us (92%)
  local copies, waits for them, and re-layouts  1.39 us (5%)
  between operations  0.69 us (3%)
    pallas_call x1, Pallas kernels, body(): pl.pallas_call(functools.partial(kernel, G, N, Q), out_shape=jax.ShapeDty...  24.4 us
    unnamed x5, local copies, waits for them, and re-layouts  1.39 us

profile of v8, /device:TPU:0, one launch (start us, length us, event | category | flops | bytes accessed | tf_op | source)
XLA Modules:
  0.0 26.4 jit_solution(3943326398974466558)
XLA Ops:
  0.0 0.0 copy-start.1
  0.7 0.0 copy-start
  0.7 0.0 copy-done.1
  0.7 0.7 %copy-done = bf16[9,8]{0,1:T(8,128)(2,1)S(1)} copy-done((bf16[9,8]{0,1:T(8,128)(2,1)S(1)}, bf16[9,8]{0,1:T(8,128)(2,1)}, u32[]{:S(2)}) %copy-start) | copy-done | bytes 168
  1.4 24.4 %shard_map.55 = f32[6,96,128]{2,1,0:T(8,128)S(1)} custom-call(f32[1,6,96,128]{3,2,1,0:T(8,128)} %part.1, bf16[8,9]{1,0:T(8,128)(2,1)S(1)} %bitcast.2, bf16[9,8,6912]{2,1,0:T(8,128)(2,1)} %bitcast.3, s32[3,8]{1,0:T(4,128)S(1)} %copy-done.1, s32[1]{0:T(128)S(6)} %copy.7.cnt_hbm), custom_call_target="tpu_custom_call" | custom-call | tf_op jit(solution)/shard_map/pallas_call | solution.py:533
  25.7 0.7 %copy.8 = f32[6,96,128]{2,1,0:T(8,128)} copy(f32[6,96,128]{2,1,0:T(8,128)S(1)} %shard_map.55) | data formatting | bytes 589824
Async XLA Ops:
  0.0 0.7 %copy-start.1 = (s32[3,8]{1,0:T(4,128)S(1)}, s32[3,8]{1,0:T(4,128)}, u32[]{:S(2)}) copy-start(s32[3,8]{1,0:T(4,128)} %off_hbm.1) | copy-start | bytes 292
  0.7 0.7 %copy-start = (bf16[9,8]{0,1:T(8,128)(2,1)S(1)}, bf16[9,8]{0,1:T(8,128)(2,1)}, u32[]{:S(2)}) copy-start(bf16[9,8]{0,1:T(8,128)(2,1)} %param.6) | copy-start | bytes 436

commit v9 on v6

--- a/solution.py
+++ b/solution.py
@@ -348,26 +348,6 @@
         def _(dj=dj, dd=dd):
             halo_copies[dj, dd].start()
 
-    for k in (1, 2, 3):
-
-        @pl.when(inside[plan[k][6]])
-        def _(k=k):
-            offset_copies[k].wait_recv()
-            for copy in block_copies[k]:
-                copy.wait_recv()
-
-        @pl.when(jnp.logical_not(inside[plan[k][6]]))
-        def _(k=k):
-            blocks[k][...] = jnp.zeros(blocks[k].shape, f32)
-            for row in range(3):
-                for s in range(slots):
-                    offs[k, row, s] = 0
-
-    unfold((1, 2, 3))
-
-    for k in (1, 2, 3):
-        place(k, False)
-
     for dj, dd in sides:
 
         @pl.when(beside[-dj, -dd])
@@ -414,6 +394,26 @@
         ).reshape(3, fw, fz)
         for i in range(3):
             dens[start + i] = (dens[start + i] + value[i]) * in_grid(start + i - HALO)
+
+    for k in (1, 2, 3):
+
+        @pl.when(inside[plan[k][6]])
+        def _(k=k):
+            offset_copies[k].wait_recv()
+            for copy in block_copies[k]:
+                copy.wait_recv()
+
+        @pl.when(jnp.logical_not(inside[plan[k][6]]))
+        def _(k=k):
+            blocks[k][...] = jnp.zeros(blocks[k].shape, f32)
+            for row in range(3):
+                for s in range(slots):
+                    offs[k, row, s] = 0
+
+    unfold((1, 2, 3))
+
+    for k in (1, 2, 3):
+        place(k, False)
 
     lanes = iota((fw, 128), 1)
     first_lane, last_lane = lanes == 0, lanes == 127

time: 24.4 us -> 27.9 us (1.14)
  Pallas kernels: 22.1 us -> 25.6 us
    pallas_call x1, Pallas kernels: 22.1 us -> 25.6 us  [body(): pl.pallas_call(functools.partial(kernel, G, N, Q), out_shape=jax.ShapeDty...]
where the time goes in v9:
time: 27.9 us; the launch traced here: 27.7 us
  Pallas kernels  25.6 us (92%)
  local copies, waits for them, and re-layouts  1.39 us (5%)
  between operations  0.69 us (2%)
    pallas_call x1, Pallas kernels, body(): pl.pallas_call(functools.partial(kernel, G, N, Q), out_shape=jax.ShapeDty...  25.6 us
    unnamed x5, local copies, waits for them, and re-layouts  1.39 us

profile of v9, /device:TPU:0, one launch (start us, length us, event | category | flops | bytes accessed | tf_op | source)
XLA Modules:
  0.0 27.7 jit_solution(16305202468226228285)
XLA Ops:
  0.0 0.0 copy-start.1
  0.7 0.0 copy-start
  0.7 0.0 copy-done.1
  0.7 0.7 %copy-done = bf16[9,8]{0,1:T(8,128)(2,1)S(1)} copy-done((bf16[9,8]{0,1:T(8,128)(2,1)S(1)}, bf16[9,8]{0,1:T(8,128)(2,1)}, u32[]{:S(2)}) %copy-start) | copy-done | bytes 168
  1.4 25.6 %shard_map.55 = f32[6,96,128]{2,1,0:T(8,128)S(1)} custom-call(f32[1,6,96,128]{3,2,1,0:T(8,128)} %part.1, bf16[8,9]{1,0:T(8,128)(2,1)S(1)} %bitcast.2, bf16[9,8,6912]{2,1,0:T(8,128)(2,1)} %bitcast.3, s32[3,8]{1,0:T(4,128)S(1)} %copy-done.1, s32[1]{0:T(128)S(6)} %copy.7.cnt_hbm), custom_call_target="tpu_custom_call" | custom-call | tf_op jit(solution)/shard_map/pallas_call | solution.py:549
  27.0 0.7 %copy.8 = f32[6,96,128]{2,1,0:T(8,128)} copy(f32[6,96,128]{2,1,0:T(8,128)S(1)} %shard_map.55) | data formatting | bytes 589824
Async XLA Ops:
  0.0 0.7 %copy-start.1 = (s32[3,8]{1,0:T(4,128)S(1)}, s32[3,8]{1,0:T(4,128)}, u32[]{:S(2)}) copy-start(s32[3,8]{1,0:T(4,128)} %off_hbm.1) | copy-start | bytes 292
  0.7 0.7 %copy-start = (bf16[9,8]{0,1:T(8,128)(2,1)S(1)}, bf16[9,8]{0,1:T(8,128)(2,1)}, u32[]{:S(2)}) copy-start(bf16[9,8]{0,1:T(8,128)(2,1)} %param.6) | copy-start | bytes 436
